TPU v7x, 32 devices: a whole 2x2x4 slice. The times are simulated.
32 devices in a mesh: groups: 1, rec: 32 (over z, y, x, core).
Axes of the slice: x: 2, y: 2, z: 4, core: 2. Of those that a mesh axis runs over, the one named last changes fastest.
Arguments:
- records: bfloat16 [4, 512, 2, 128], P(None, ('groups', 'rec')), may hold values from -6 to 6
- dest: int32 [512, 4], P('groups'), may hold values from 0 to 31, as said below
- w_in: bfloat16 [64, 36], replicated, may hold values from -1 to 1
- b_in: float32 [64], replicated, may hold values from -3 to 3
- w_mid: bfloat16 [64, 64], replicated, may hold values from -0.75 to 0.75
- b_mid: float32 [64], replicated, may hold values from -3 to 3
- w_out: bfloat16 [64, 36], replicated, may hold values from -0.25 to 0.25
Outputs:
- residual: float32 [4, 512, 2, 128], P(None, ('groups', 'rec'))
- grad_w_in: float32 [64, 36], P('groups')
- grad_b_in: float32 [64], P('groups')
- grad_w_mid: float32 [64, 64], P('groups')
- grad_b_mid: float32 [64], P('groups')
- grad_w_out: float32 [64, 36], P('groups')
Inputs may be any that keep to these rules, and one draw needn't show every extreme that they name: `dest`: from the 16 blocks of one record device at most 2 copies go to one owner; in every draw one owner receives exactly 2 copies from every record device.
All inputs are finite; a program needn't handle non-finite values.
Results may differ from a plain program's by a relative error of at most 0.0005.
The roundings to bfloat16 on the way count: a program that leaves them out, or rounds other values in their place, can miss the bound.
Values may be sent and summed in bfloat16 or wider, within the bound.
No kernel may reach another device: no remote copies, remote signals or barrier semaphores. Data moves between devices by JAX's collectives and lax.ppermute only.
A program may use at most 192 MiB of HBM per device.

v0:
```python
import functools
import math

import jax
import jax.numpy as jnp
from jax import lax
from jax.experimental import pallas as pl
from jax.experimental.pallas import tpu as pltpu
from jax.sharding import PartitionSpec as P

CAP = 2
VMEM = pl.BlockSpec(memory_space=pltpu.VMEM)
RESIDENT = 24 << 20


def run(start, step, end, steps, blocked, table):
    copy = pltpu.make_async_copy(*table)

    def begin():
        copy.start()
        start()
        copy.wait()

    if blocked:
        n = pl.program_id(0)
        pl.when(n == 0)(begin)
        step(n, 0)
        pl.when(n == steps - 1)(end)
        return
    begin()
    lax.fori_loop(0, steps, lambda n, carry: step(n, n), None)
    end()


def group_of(owners):
    for size in (32, 16, 8, 4, 2):
        if owners % size == 0:
            return size
    return 1


def fill_table(table, pieces, tiles, flip, fill):
    for n, piece in enumerate(pieces):
        x = piece[...].astype(jnp.float32)
        x = jnp.concatenate([x, x], axis=1)
        samples = x.shape[2]
        row = lax.broadcasted_iota(jnp.int32, x.shape, 1)
        lane = lax.broadcasted_iota(jnp.int32, x.shape, 2)
        earlier = row >= 4 if flip else row < 4
        sides = jnp.where(earlier, pltpu.roll(x, 1, 2), pltpu.roll(x, samples - 1, 2))
        sides = jnp.where(lane == jnp.where(earlier, 0, samples - 1), 0.0, sides)
        rest = jnp.where(row < 4, x, fill)
        table[pl.ds(n * tiles, tiles)] = jnp.concatenate([sides, rest], axis=1).astype(jnp.bfloat16)
    last, count = len(pieces) * tiles, table.shape[0]
    row = lax.broadcasted_iota(jnp.int32, (count - last, *table.shape[1:]), 1)
    table[pl.ds(last, count - last)] = jnp.where(row < 12, 0.0, fill).astype(jnp.bfloat16)


def act(y):
    t = jnp.tanh(y)
    q = 1.0 + t
    a = y * q
    return t, q, a


def lines_of(idx, own, halo, owners):
    lines = []
    for e in owners:
        line = []
        for r in range(4):
            held = own if r in (1, 2) else halo
            line += [None, None] if held is None else [held[idx[r, e]], held[idx[r, e] + 1]]
        lines.append(line)
    return lines


def stack(lines, traces, flip):
    return jnp.concatenate(
        [
            jnp.concatenate(
                [line[h + 1 + (2 - i if flip else i)] for line in lines for h in traces], axis=1
            )
            for i in range(3)
        ],
        axis=0,
    )


def pipeline(pieces, *stages):
    held = [None] * pieces
    for tick in range(pieces + len(stages) - 1):
        for behind in reversed(range(len(stages))):
            k = tick - behind
            if 0 <= k < pieces:
                held[k] = stages[behind](k, held[k])


def layer(w, inputs):
    t, q, a = act(jnp.dot(w[...], inputs, preferred_element_type=jnp.float32))
    return a, q + a * (1.0 - t)


def with_ones(a1):
    return jnp.concatenate([a1, jnp.ones((16, a1.shape[1]), jnp.bfloat16)], axis=0)


def forward_inner(
    group, blocked, slots, mine, w1, w2, own, a1_ref, a2_ref, d1_ref, d2_ref, idx, sem,
):
    owners = lax.axis_size("rec")

    def start():
        fill_table(own, (mine,), mine.shape[0], False, 1.0)

    def step(n, block):
        sub = group
        width = sub * 2 * mine.shape[2]

        def first(k, _):
            es = [n * group + k * sub + u for u in range(sub)]
            at = slice(k * width, (k + 1) * width)
            a, d = layer(w1, stack(lines_of(idx, own, None, es), (1, 2), False))
            a1_ref[block, :, at] = a.astype(jnp.bfloat16)
            d1_ref[block, :, at] = d
            return a.astype(jnp.bfloat16)

        def second(k, a1):
            at = slice(k * width, (k + 1) * width)
            a, d = layer(w2, with_ones(a1))
            a2_ref[block, :, at] = a.astype(jnp.bfloat16)
            d2_ref[block, :, at] = d

        pipeline(group // sub, first, second)

    run(start, step, lambda: None, owners // group, blocked, (slots, idx, sem))


def forward_outer(
    group, blocked, slots, near, mine, far, own, w1, w2, w3, inner,
    res, g, halo, a1_ref, a2_ref, d1_ref, d2_ref, est, idx, sem,
):
    tiles, parts, samples = mine.shape
    count = lax.axis_size("rec")
    me = lax.axis_index("rec")
    has_left = (me > 0).astype(jnp.float32)
    has_right = (me < count - 1).astype(jnp.float32)
    lane = lax.broadcasted_iota(jnp.int32, (8, samples), 1)
    low = (lane > 0).astype(jnp.float32)
    high = (lane < samples - 1).astype(jnp.float32)

    def start():
        fill_table(halo, (near, far), tiles, False, 1.0)

    def step(n, block):
        cut = lambda x, k: x[:, k * samples : (k + 1) * samples]

        sub = min(8, group)
        own_part = lambda x: jnp.concatenate(
            [x[:, (u * 4 + 1) * samples : (u * 4 + 3) * samples] for u in range(sub)], axis=1
        )
        width = sub * 2 * samples

        def first(k, _):
            lines = lines_of(idx, own, halo, [n * group + k * sub + u for u in range(sub)])
            at = slice(k * width, (k + 1) * width)
            a, d = layer(w1, stack(lines, (-1, 0, 3, 4), False))
            a1 = a.astype(jnp.bfloat16)
            a1_ref[block, :, at] = own_part(a1)
            d1_ref[block, :, at] = own_part(d)
            return a1

        def second(k, a1):
            at = slice(k * width, (k + 1) * width)
            a, d = layer(w2, with_ones(a1))
            d2_ref[block, :, at] = own_part(d)
            a2_ref[block, :, at] = own_part(a).astype(jnp.bfloat16)
            rows = []
            for u in range(sub):
                row = [cut(a, u * 4 + h) for h in range(4)]
                row = [row[0] * has_left, row[1], row[2], row[3] * has_right]
                row = [part.astype(jnp.bfloat16) for part in row]
                within = [cut(inner.at[block], (k * sub + u) * 2 + h) for h in range(2)]
                rows.append(row[0:2] + within + row[2:4])
            return rows

        def third(k, rows):
            rhs = [
                jnp.concatenate([part for row in rows for part in row[i : i + 4]], axis=1)
                for i in range(3)
            ]
            terms = jnp.dot(
                w3[...], jnp.concatenate(rhs, axis=0), preferred_element_type=jnp.float32
            )
            for h in range(sub * 4):
                part = cut(terms, h)
                total = (
                    part[8:16]
                    + pltpu.roll(part[0:8], 1, 1) * low
                    + pltpu.roll(part[16:24], samples - 1, 1) * high
                )
                at = (n * group + k * sub) * 4 + h
                est[at] = total.astype(jnp.bfloat16).astype(jnp.float32)

        pipeline(group // sub, first, second, third)

    def end():
        for c in range(tiles // 2):
            at = [idx[4 + v, tiles // 2 + c] for v in range(4)]
            for k in range(2):
                total = (est[at[0] + k] + est[at[1] + k]) + (est[at[2] + k] + est[at[3] + k])
                value = total[0:parts] - mine[c * 2 + k].astype(jnp.float32)
                for o in range(parts):
                    res[o, c, k : k + 1, :] = value[o : o + 1]
                g[c * 2 + k] = value.astype(jnp.bfloat16)

    run(start, step, end, count // group, blocked, (slots, idx, sem))


def weight_terms(acc, pieces, width, fields_of, inputs_of, wo, wm, saved):
    channels = wm.shape[0]
    a1, a2, d1, d2 = saved
    of = lambda ref, k: ref[:, k * width : (k + 1) * width]

    def first(k, _):
        fields = fields_of(k)
        da2 = jnp.dot(wo[...], fields, preferred_element_type=jnp.float32)
        acc[0:48, :] += product(fields, of(a2, k), (1, 1))
        return (da2 * of(d2, k)).astype(jnp.bfloat16)

    def second(k, dz2):
        da1 = jnp.dot(wm[...], dz2, preferred_element_type=jnp.float32)
        acc[48 : 64 + channels, :] += product(with_ones(of(a1, k)), dz2, (1, 1))
        return (da1 * of(d1, k)).astype(jnp.bfloat16)

    def third(k, dz1):
        acc[64 + channels : 112 + channels, :] += product(inputs_of(k), dz1, (1, 1))

    pipeline(pieces, first, second, third)


def backward_inner(
    group, blocked, slots, mine, wo, wm, own, a1_ref, a2_ref, d1_ref, d2_ref, gown, acc,
    idx, sem,
):
    owners = lax.axis_size("rec")

    def start():
        fill_table(gown, (mine,), mine.shape[0], True, 0.0)
        acc[...] = jnp.zeros_like(acc)

    def step(n, block):
        sub = group
        es = lambda k: [n * group + k * sub + u for u in range(sub)]
        weight_terms(
            acc, group // sub, sub * 2 * mine.shape[2],
            lambda k: stack(lines_of(idx, gown, None, es(k)), (1, 2), True),
            lambda k: stack(lines_of(idx, own, None, es(k)), (1, 2), False),
            wo, wm, [ref.at[block] for ref in (a1_ref, a2_ref, d1_ref, d2_ref)],
        )

    run(start, step, lambda: None, owners // group, blocked, (slots, idx, sem))


def backward_outer(
    group, blocked, slots, near, far, wo, wm, own, halo, gown, sums, a1_ref, a2_ref, d1_ref, d2_ref,
    out, ghalo, acc, idx, sem,
):
    owners = lax.axis_size("rec")
    channels = wm.shape[0]
    taps = 9 * near.shape[1]

    def start():
        fill_table(ghalo, (near, far), near.shape[0], True, 0.0)
        acc[...] = sums[...]

    def step(n, block):
        sub = group
        es = lambda k: [n * group + k * sub + u for u in range(sub)]
        weight_terms(
            acc, group // sub, sub * 2 * near.shape[2],
            lambda k: stack(lines_of(idx, gown, ghalo, es(k)), (0, 3), True),
            lambda k: stack(lines_of(idx, own, halo, es(k)), (0, 3), False),
            wo, wm, [ref.at[block] for ref in (a1_ref, a2_ref, d1_ref, d2_ref)],
        )

    def end():
        first, half = 64 + channels, channels // 2
        low, high = slice(0, channels), slice(channels, 2 * channels)
        for k in range(taps):
            at = k % 9 // 3 * 16 + k % 3 * 2 % 3 * 4 + k // 9
            out[half + k : half + k + 1, low] = acc[first + at : first + at + 1, :]
            out[half + k : half + k + 1, high] = acc[at : at + 1, :]
        middle = acc[48 : 48 + channels, :].T
        out[0:half, low] = middle[0:half]
        out[0:half, high] = middle[half:channels]
        out[half + taps : half + taps + 1, low] = acc[first + 28 : first + 29, :]
        out[half + taps : half + taps + 1, high] = acc[48 + channels : 49 + channels, :]
        rest = out.shape[0] - half - taps - 1
        out[half + taps + 1 :, :] = jnp.zeros((rest, 2 * channels), jnp.float32)

    run(start, step, end, owners // group, blocked, (slots, idx, sem))


def finish_kernel(scale, *refs):
    terms, (g_in, g_bin, g_mid, g_bmid, g_out, held) = refs[:-6], refs[-6:]
    values = [ref[...] for ref in terms]
    while len(values) > 1:
        values = [values[k] + values[k + 1] for k in range(0, len(values), 2)]
    held[...] = values[0] * scale
    channels = g_mid.shape[0]
    half, taps = channels // 2, g_in.shape[0]
    low, high = slice(0, channels), slice(channels, 2 * channels)
    g_mid[0:half] = held[0:half, low]
    g_mid[half:channels] = held[0:half, high]
    g_in[...] = held[half : half + taps, low]
    g_out[...] = held[half : half + taps, high]
    g_bin[...] = held[half + taps : half + taps + 1, low]
    g_bmid[...] = held[half + taps : half + taps + 1, high]


def halves(b):
    high = b.astype(jnp.bfloat16).astype(jnp.float32)
    rest = b - high
    mid = rest.astype(jnp.bfloat16).astype(jnp.float32)
    return [high, mid, rest - mid]


def one_hot(a, b):
    return (a == b).astype(jnp.float32).astype(jnp.bfloat16)


def iota(shape, dim):
    return lax.broadcasted_iota(jnp.int32, shape, dim)


def product(a, b, over):
    return lax.dot_general(
        a, b, dimension_numbers=(((over[0],), (over[1],)), ((), ())),
        preferred_element_type=jnp.float32,
    )


def prep_kernel(blocks, *refs):
    args, (idx, w1, w2, w3, wo, wm, rows), held, sems = refs[:6], refs[6:13], refs[13:19], refs[19]
    copies = [
        pltpu.make_async_copy(src, dst, sems.at[n]) for n, (src, dst) in enumerate(zip(args, held))
    ]
    for copy in copies:
        copy.start()
    for copy in copies:
        copy.wait()
    dest, w_in, b_in, w_mid, b_mid, w_out = held
    count = lax.axis_size("rec")
    me = lax.axis_index("rec")
    ves, total = dest.shape
    channels = w_mid.shape[0]
    at = lax.rem((count + 1 - me) * blocks, total)
    wide = jnp.concatenate([dest[...], jnp.zeros((8 - ves, total), jnp.int32)], axis=0)
    near = pltpu.roll(wide, at, 1)[:, 0:128]
    lane = iota((8, 128), 1)
    low = jnp.where(me > 0, 0, blocks)
    high = jnp.where(me < count - 1, 3 * blocks, 2 * blocks)
    near = jnp.where((lane >= low) & (lane < high), near, -1)
    owner = iota((count, 128), 0)
    hits = [(near[v : v + 1] == owner).astype(jnp.float32) for v in range(ves)]
    before = iota((128, 128), 0)
    after = iota((128, 128), 1)
    segment = (after >= blocks).astype(jnp.int32) + (after >= 2 * blocks).astype(jnp.int32)
    tri = ((before < after) & (before >= segment * blocks)).astype(jnp.float32).astype(jnp.bfloat16)
    rank = product((hits[0] + hits[1] + hits[2] + hits[3]).astype(jnp.bfloat16), tri, (1, 0))
    zeroth = jnp.zeros((count, 128), jnp.float32)
    first = jnp.zeros((count, 128), jnp.float32)
    for v in range(ves):
        zeroth += hits[v] * (rank == 0.0).astype(jnp.float32)
        first += hits[v] * (rank == 1.0).astype(jnp.float32)
        item = jnp.sum(hits[v] * rank, axis=0, keepdims=True)
        idx[4 + v : 5 + v, 0:128] = near[v : v + 1] * 4 + item.astype(jnp.int32) * 2
        rank = rank + hits[v]
    line = iota((8, 128), 0)
    inside = lambda k: (lane >= k * blocks) & (lane < (k + 1) * blocks)
    odd = lax.rem(me, 2)
    left = 2 * lane + 2 * blocks * (1 - odd) - 4 * blocks
    middle = 2 * (lane - blocks) - 2 * blocks
    right = 2 * (lane - 2 * blocks) + 2 * blocks * odd - 4 * blocks
    put = lambda r, k, place: jnp.where((line == r) & inside(k), place, 0)
    pick = product(
        (put(0, 0, left) + put(2, 1, middle)).astype(jnp.float32).astype(jnp.bfloat16),
        first.astype(jnp.bfloat16),
        (1, 1),
    ) + product(
        (put(1, 1, middle) + put(3, 2, right)).astype(jnp.float32).astype(jnp.bfloat16),
        zeroth.astype(jnp.bfloat16),
        (1, 1),
    )
    empty = jnp.where((line == 0) | (line == 3), 4 * blocks, 2 * blocks)[0:4, 0:1]
    idx[0:4, 0:count] = pick[0:4].astype(jnp.int32) + empty

    taps = w_in.shape[0]
    row, col = iota((48, 40), 0), iota((48, 40), 1)
    tap, extra = row & 15, (row & 15) - 12
    place = (row >> 2) & 3
    target = (row & 3) * 9 + 3 * (row >> 4) + jnp.where(place == 0, 0, 3 - place)
    target = jnp.where(tap < 12, target, jnp.where((row >> 4) == 1, taps + extra, -1))
    order = one_hot(col, target)
    rows[...] = jnp.zeros_like(rows)
    rows[0:taps, :] = w_in[...].astype(jnp.float32)
    for n, part in enumerate(halves(b_in[...])):
        rows[taps + n : taps + n + 1, :] = part
    w1[...] = (0.5 * product(rows[...].astype(jnp.bfloat16), order, (0, 1))).astype(jnp.bfloat16)
    rows[...] = jnp.zeros_like(rows)
    for n, part in enumerate(halves(b_mid[...])):
        rows[n : n + 1, :] = part
    row, col = iota((40, channels + 16), 0), iota((40, channels + 16), 1)
    bias = product(rows[...].astype(jnp.bfloat16), one_hot(col, row + channels), (0, 0))
    row, col = iota((channels, channels + 16), 0), iota((channels, channels + 16), 1)
    w2[...] = (0.5 * (product(w_mid[...], one_hot(row, col), (1, 0)) + bias)).astype(jnp.bfloat16)
    rows[...] = jnp.zeros_like(rows)
    rows[0:taps, :] = w_out[...].astype(jnp.float32)
    outs = rows[...].astype(jnp.bfloat16)
    wo[...] = (0.5 * product(outs, order, (0, 1))).astype(jnp.bfloat16)
    row, col = iota((24, 40), 0), iota((24, 40), 1)
    for i in range(3):
        target = jnp.where((row & 7) < 4, (row & 3) * 9 + 3 * i + (row >> 3), -1)
        part = product(one_hot(col, target), outs, (1, 0))
        w3[:, i * channels : (i + 1) * channels] = part.astype(jnp.bfloat16)
    eye = one_hot(iota((channels, channels), 0), iota((channels, channels), 1))
    wm[...] = (0.5 * product(w_mid[...], eye, (0, 0))).astype(jnp.bfloat16)


def local(records, dest, w_in, b_in, w_mid, b_mid, w_out):
    count = lax.axis_size("rec")
    me = lax.axis_index("rec")
    parts, blocks, traces, samples = records.shape
    ves = dest.shape[1]
    tiles = blocks * traces
    channels = w_in.shape[0]
    group = group_of(count)
    steps = count // group
    width = group * 2 * samples
    far = [(s, s + 1) for s in range(1, count - 1, 2)]
    far += [(b, a) for a, b in far]
    near = [(s, s + 1) for s in range(0, count - 1, 2)]
    near += [(b, a) for a, b in near]

    flat = records.transpose(1, 2, 0, 3).reshape(tiles, parts, samples)
    from_far = lax.ppermute(flat, "rec", far)
    from_near = lax.ppermute(flat, "rec", near)

    f32, bf16 = jnp.float32, jnp.bfloat16
    shape = (steps, channels, width)
    blocked = 24 * math.prod(shape) > RESIDENT
    saved = [
        jax.ShapeDtypeStruct(shape, kind) if blocked else pltpu.VMEM(shape, kind)
        for kind in (bf16, bf16, f32, f32)
    ]
    held = [VMEM] * 4
    if blocked:
        held = [pl.BlockSpec((1, channels, width), lambda n: (n, 0, 0))] * 4
    grid = (steps,) if blocked else ()
    params = pltpu.CompilerParams(vmem_limit_bytes=16 << 20)
    args = (
        dest.T, w_in.T, b_in.reshape(1, channels), w_mid, b_mid.reshape(1, channels), w_out.T
    )
    idx, w1, w2, w3, wo, wm = pl.pallas_call(
        functools.partial(prep_kernel, blocks),
        out_shape=[jax.ShapeDtypeStruct((8, max(128, count)), jnp.int32)]
        + [
            jax.ShapeDtypeStruct(size, bf16)
            for size in (
                (channels, 48), (channels, channels + 16), (24, 3 * channels), (channels, 48),
                (channels, channels),
            )
        ],
        in_specs=[pl.BlockSpec(memory_space=pltpu.HBM)] * 6,
        out_specs=[VMEM] * 6,
        scratch_shapes=[pltpu.VMEM((40, channels), f32)]
        + [pltpu.VMEM(arg.shape, arg.dtype) for arg in args]
        + [pltpu.SemaphoreType.DMA((6,))],
        compiler_params=params,
        name="prepare",
    )(*[pltpu.with_memory_space_constraint(arg, pltpu.HBM) for arg in args])
    def table(pieces, kind):
        return pltpu.VMEM((pieces * tiles + 2, 16, samples), kind)

    def call(kernel, ins, outs, scratch, args, name, owned):
        return pl.pallas_call(
            functools.partial(kernel, group, blocked),
            grid=grid,
            out_shape=outs[0] + saved * outs[1],
            in_specs=[VMEM] * (1 + ins[0]) + held[:1] * ins[1],
            out_specs=[VMEM] * len(outs[0]) + held * outs[1],
            scratch_shapes=scratch + [pltpu.SMEM(idx.shape, idx.dtype), pltpu.SemaphoreType.DMA],
            compiler_params=params,
            cost_estimate=pl.CostEstimate(
                flops=2 * owned * count * samples * channels * (3 * channels),
                bytes_accessed=owned * count * samples * channels * 12,
                transcendentals=0,
            ),
            name=name,
        )(*args)

    total = (112 + channels, channels)
    rows = (channels // 2 + 9 * parts + 1 + 7) // 8 * 8
    own, *inner = call(
        forward_inner, (3, 0), ([table(1, bf16)], 1), [],
        (idx, flat, w1, w2), "forward_inner", 2,
    )
    res, g, halo, *outer = call(
        forward_outer, (7, 1),
        (
            [
                jax.ShapeDtypeStruct(records.shape, f32),
                jax.ShapeDtypeStruct((tiles, parts, samples), bf16),
                table(2, bf16),
            ],
            1,
        ),
        [pltpu.VMEM((count * 4, 8, samples), f32)],
        (idx, from_near, flat, from_far, own, w1, w2, w3, inner[1]), "forward_outer", 4,
    )
    g_far = lax.ppermute(g, "rec", far)
    g_near = lax.ppermute(g, "rec", near)
    gown, part = call(
        backward_inner, (4, 4), ([table(1, bf16), pltpu.VMEM(total, f32)], 0), [],
        (idx, g, wo, wm, own, *inner), "backward_inner", 2,
    )
    (sums,) = call(
        backward_outer, (8, 4), ([jax.ShapeDtypeStruct((rows, 2 * channels), f32)], 0),
        [table(2, bf16), pltpu.VMEM(total, f32)],
        (idx, g_near, g_far, wo, wm, own, halo, gown, part, *outer), "backward_outer", 2,
    )

    if count & (count - 1):
        terms = [lax.psum(sums, "rec")]
    else:
        terms = [sums]
        at = 1
        while at < count:
            wide = 4 if at > 1 and 4 * at <= count else 2
            value = terms[0]
            if len(terms) == 2:
                value = terms[0] + terms[1]
            if len(terms) == 4:
                value = (terms[0] + terms[1]) + (terms[2] + terms[3])
            terms = [value] + [
                lax.ppermute(value, "rec", [(s, s ^ (k * at)) for s in range(count)])
                for k in range(1, wide)
            ]
            at *= wide

    scale = 1.0 / math.sqrt(parts * blocks * count * traces * samples)
    g_in, g_bin, g_mid, g_bmid, g_out = pl.pallas_call(
        functools.partial(finish_kernel, scale),
        out_shape=[
            jax.ShapeDtypeStruct(shape, f32)
            for shape in (
                (parts * 9, channels), (1, channels), (channels, channels), (1, channels),
                (parts * 9, channels),
            )
        ],
        in_specs=[VMEM] * len(terms),
        out_specs=[VMEM] * 5,
        scratch_shapes=[pltpu.VMEM(sums.shape, f32)],
        compiler_params=params,
        name="finish",
    )(*terms)
    return (
        res,
        g_in.T,
        g_bin.reshape(channels),
        g_mid,
        g_bmid.reshape(channels),
        g_out.T,
    )


def solution(mesh):
    return jax.shard_map(
        local,
        mesh=mesh,
        in_specs=(
            P(None, ("groups", "rec"), None, None),
            P("groups", None),
            P(),
            P(),
            P(),
            P(),
            P(),
        ),
        out_specs=(
            P(None, ("groups", "rec"), None, None),
            P("groups", None),
            P("groups"),
            P("groups", None),
            P("groups"),
            P("groups", None),
        ),
        check_vma=False,
    )
```

profile of v0, /device:TPU:0, one launch (start us, length us, event | category | flops | bytes accessed | tf_op | source)
XLA Modules:
  0.0 39.5 jit_solution(10491470869284437766)
XLA Ops:
  0.6 0.8 %copy.13 = bf16[16,2,4,128]{3,2,1,0:T(4,128)(2,1)S(1)} copy(bf16[16,2,4,128]{3,1,0,2:T(2,128)(2,1)} %bitcast.15) | data formatting | bytes 65536 | tf_op jit(solution)/shard_map/transpose | solution.py:445
  1.4 0.7 %collective-permute-start.1 = (bf16[32,4,128]{2,1,0:T(4,128)(2,1)S(1)}, bf16[32,4,128]{2,1,0:T(4,128)(2,1)S(1)}, u32[]{:S(2)}, u32[]{:S(2)}) collective-permute-start(bf16[32,4,128]{2,1,0:T(4,128)(2,1)S(1)} %bitcast.11), channel_id=1, source_target_pairs={{1,2},{3,4},{5,6},{7,8},{9,10},{11,12},{13,14},{15,16},{17,18},{19... | collective-permute-start | bytes 98312 | tf_op jit(solution)/shard_map/ppermute | solution.py:446
  2.1 4.4 %collective-permute-start = (bf16[32,4,128]{2,1,0:T(4,128)(2,1)S(1)}, bf16[32,4,128]{2,1,0:T(4,128)(2,1)S(1)}, u32[]{:S(2)}, u32[]{:S(2)}) collective-permute-start(bf16[32,4,128]{2,1,0:T(4,128)(2,1)S(1)} %bitcast.12), channel_id=1, source_target_pairs={{0,1},{2,3},{4,5},{6,7},{8,9},{10,11},{12,13},{14,15},{16,17},{18,... | collective-permute-start | bytes 98312 | tf_op jit(solution)/shard_map/ppermute | solution.py:447
  6.4 1.3 %prepare.1 = (s32[8,128]{1,0:T(8,128)S(1)}, bf16[64,48]{1,0:T(8,128)(2,1)S(1)}, bf16[64,80]{1,0:T(8,128)(2,1)S(1)}, bf16[24,192]{1,0:T(8,128)(2,1)S(1)}, bf16[64...) custom-call(s32[4,512]{1,0:T(4,128)} %bitcast.18, bf16[36,64]{1,0:T(8,128)(2,1)} %bitcast.16, f32[1,64]{1,0:T(1,128)} %bitcast.19, ...), custom_call_target="tpu_custom_call" | custom-call | tf_op jit(solution)/shard_map/prepare/pallas_call | solution.py:464
  7.7 2.1 %forward_inner.1 = (bf16[34,16,128]{2,1,0:T(8,128)(2,1)S(1)}, bf16[1,64,8192]{2,1,0:T(8,128)(2,1)S(1)}, bf16[1,64,8192]{2,1,0:T(8,128)(2,1)S(1)}, f32[1,64,8192]{2,1,0:T(8,128)S(1)}, f32[1,64,8192]{2,1,0:T(8,128)S(1)}) custom-call(s32[8,128]{1,0:T(8,128)S(1)} %get-tuple-element.31.slots, bf16[32,4,128]{2,1,0:T(4,128)(2,1)S(1)} %bitcast.13, ...), custom_call_target="tpu_custom_call" | custom-call | flops 201326592 | bytes 6291456 | tf_op jit(solution)/shard_map/forward_inner/pallas_call | solution.py:486
  9.8 0.0 collective-permute-done.1.far
  9.8 0.0 collective-permute-done.near
  9.8 4.1 %forward_outer.1 = (f32[4,16,2,128]{3,2,1,0:T(2,128)}, bf16[32,4,128]{2,1,0:T(4,128)(2,1)S(1)}, bf16[66,16,128]{2,1,0:T(8,128)(2,1)S(1)}, bf16[1,64,8192]{2,1,0:...) custom-call(s32[8,128]{1,0:T(8,128)S(1)} %get-tuple-element.31.slots, ...), custom_call_target="tpu_custom_call" | custom-call | flops 402653184 | bytes 12582912 | tf_op jit(solution)/shard_map/forward_outer/pallas_call | solution.py:486
  13.9 0.7 %collective-permute-start.3 = (bf16[32,4,128]{2,1,0:T(4,128)(2,1)S(1)}, bf16[32,4,128]{2,1,0:T(4,128)(2,1)S(1)}, u32[]{:S(2)}, u32[]{:S(2)}) collective-permute-start(bf16[32,4,128]{2,1,0:T(4,128)(2,1)S(1)} %get-tuple-element.38.mine), channel_id=1, source_target_pairs={{1,2},{3,4},{5,6},{7,8},{9,10},{11,12},{13,14},{15,16},{17,18},{19... | collective-permute-start | bytes 98312 | tf_op jit(solution)/shard_map/ppermute | solution.py:521
  14.6 2.9 %collective-permute-start.2 = (bf16[32,4,128]{2,1,0:T(4,128)(2,1)S(1)}, bf16[32,4,128]{2,1,0:T(4,128)(2,1)S(1)}, u32[]{:S(2)}, u32[]{:S(2)}) collective-permute-start(bf16[32,4,128]{2,1,0:T(4,128)(2,1)S(1)} %get-tuple-element.38.mine), channel_id=1, source_target_pairs={{0,1},{2,3},{4,5},{6,7},{8,9},{10,11},{12,13},{14,15},{16,17},{18,... | collective-permute-start | bytes 98312 | tf_op jit(solution)/shard_map/ppermute | solution.py:522
  17.5 2.2 %backward_inner.1 = (bf16[34,16,128]{2,1,0:T(8,128)(2,1)S(1)}, f32[176,64]{1,0:T(8,128)S(1)}) custom-call(s32[8,128]{1,0:T(8,128)S(1)} %get-tuple-element.31.slots, bf16[32,4,128]{2,1,0:T(4,128)(2,1)S(1)} %get-tuple-element.38.mine, bf16[64,48]{1,0:T(8,128)(2,1)S(1)} %get-tuple-element.39.wo, bf16[64,64]{1,0:T(8,128)(2,1)S(1)} %get-tuple-element.40.wm, ...), custom_call_target="tpu_custom_call" | custom-call | flops 201326592 | bytes 6291456 | tf_op jit(solution)/shard_map/backward_inner/pallas_call | solution.py:486
  19.7 0.0 collective-permute-done.3.far
  19.7 0.0 collective-permute-done.2.near
  19.8 2.3 %backward_outer.1 = f32[72,128]{1,0:T(8,128)S(1)} custom-call(s32[8,128]{1,0:T(8,128)S(1)} %get-tuple-element.31.slots, bf16[32,4,128]{2,1,0:T(4,128)(2,1)S(1)} %collective-permute-done.2.near, bf16[32,4,128]{2,1,0:T(4,128)(2,1)S(1)} %collective-permute-done.3.far, bf16[64,48]{1,0:T(8,128)(2,1)S(1)} %get-tuple-element.39.wo, ...), custom_call_target="tpu_custom_call" | custom-call | flops 201326592 | bytes 6291456 | tf_op jit(solution)/shard_map/backward_outer/pallas_call | solution.py:486
  22.0 0.1 collective-permute-start.4
  22.1 1.2 %collective-permute-done.4 = f32[72,128]{1,0:T(8,128)S(1)} collective-permute-done((f32[72,128]{1,0:T(8,128)S(1)}, f32[72,128]{1,0:T(8,128)S(1)}, u32[]{:S(2)}, u32[]{:S(2)}) %collective-permute-start.4) | collective-permute-done | bytes 36896 | tf_op jit(solution)/shard_map/ppermute | solution.py:546
  23.3 3.3 %collective-permute-start.7 = (f32[72,128]{1,0:T(8,128)S(1)}, f32[72,128]{1,0:T(8,128)S(1)}, u32[]{:S(2)}, u32[]{:S(2)}) collective-permute-start(f32[72,128]{1,0:T(8,128)S(1)} %add.12), channel_id=1, source_target_pairs={{0,6},{1,7},{2,4},{3,5},{4,2},{5,3},{6,0},{7,1},{8,14},{9,15},{10,... | collective-permute-start | bytes 110600 | tf_op jit(solution)/shard_map/ppermute | solution.py:546
  26.6 0.0 collective-permute-start.6
  26.6 0.6 %collective-permute-start.5 = (f32[72,128]{1,0:T(8,128)S(1)}, f32[72,128]{1,0:T(8,128)S(1)}, u32[]{:S(2)}, u32[]{:S(2)}) collective-permute-start(f32[72,128]{1,0:T(8,128)S(1)} %add.12), channel_id=1, source_target_pairs={{0,2},{1,3},{2,0},{3,1},{4,6},{5,7},{6,4},{7,5},{8,10},{9,11},{10,... | collective-permute-start | bytes 110600 | tf_op jit(solution)/shard_map/ppermute | solution.py:546
  27.3 1.4 %collective-permute-done.7 = f32[72,128]{1,0:T(8,128)S(1)} collective-permute-done((f32[72,128]{1,0:T(8,128)S(1)}, f32[72,128]{1,0:T(8,128)S(1)}, u32[]{:S(2)}, u32[]{:S(2)}) %collective-permute-start.7) | collective-permute-done | bytes 36896 | tf_op jit(solution)/shard_map/ppermute | solution.py:546
  28.6 2.0 %collective-permute-done.6 = f32[72,128]{1,0:T(8,128)S(1)} collective-permute-done((f32[72,128]{1,0:T(8,128)S(1)}, f32[72,128]{1,0:T(8,128)S(1)}, u32[]{:S(2)}, u32[]{:S(2)}) %collective-permute-start.6) | collective-permute-done | bytes 36896 | tf_op jit(solution)/shard_map/ppermute | solution.py:546
  30.6 0.0 collective-permute-done.5
  30.6 3.3 %collective-permute-start.10 = (f32[72,128]{1,0:T(8,128)S(1)}, f32[72,128]{1,0:T(8,128)S(1)}, u32[]{:S(2)}, u32[]{:S(2)}) collective-permute-start(f32[72,128]{1,0:T(8,128)S(1)} %add_add_fusion.refs_0_), channel_id=1, source_target_pairs={{0,24},{1,25},{2,26},{3,27},{4,28},{5,29},{6,30},{7,31},{8,16},{9,... | collective-permute-start | bytes 110600 | tf_op jit(solution)/shard_map/ppermute | solution.py:546
  33.9 0.0 collective-permute-start.9
  33.9 1.1 %collective-permute-start.8 = (f32[72,128]{1,0:T(8,128)S(1)}, f32[72,128]{1,0:T(8,128)S(1)}, u32[]{:S(2)}, u32[]{:S(2)}) collective-permute-start(f32[72,128]{1,0:T(8,128)S(1)} %add_add_fusion.refs_0_), channel_id=1, source_target_pairs={{0,8},{1,9},{2,10},{3,11},{4,12},{5,13},{6,14},{7,15},{8,0},{9,1},... | collective-permute-start | bytes 110600 | tf_op jit(solution)/shard_map/ppermute | solution.py:546
  35.1 1.4 %collective-permute-done.10.refs_3_ = f32[72,128]{1,0:T(8,128)S(1)} collective-permute-done((f32[72,128]{1,0:T(8,128)S(1)}, f32[72,128]{1,0:T(8,128)S(1)}, u32[]{:S(2)}, u32[]{:S(2)}) %collective-permute-start.10) | collective-permute-done | bytes 36896 | tf_op jit(solution)/shard_map/ppermute | solution.py:546
  36.5 2.3 %collective-permute-done.9.refs_2_ = f32[72,128]{1,0:T(8,128)S(1)} collective-permute-done((f32[72,128]{1,0:T(8,128)S(1)}, f32[72,128]{1,0:T(8,128)S(1)}, u32[]{:S(2)}, u32[]{:S(2)}) %collective-permute-start.9) | collective-permute-done | bytes 36896 | tf_op jit(solution)/shard_map/ppermute | solution.py:546
  38.8 0.0 collective-permute-done.8.refs_1_
  38.8 0.7 %finish.1 = (f32[36,64]{1,0:T(8,128)}, f32[1,64]{1,0:T(1,128)}, f32[64,64]{1,0:T(8,128)}, f32[1,64]{1,0:T(1,128)}, f32[36,64]{1,0:T(8,128)}) custom-call(f32[72,128]{1,0:T(8,128)S(1)} %add_add_fusion.refs_0_, f32[72,128]{1,0:T(8,128)S(1)} %collective-permute-done.8.refs_1_, f32[72,128]{1,0:T(8,128)S(1)} %collective-permute-done.9.refs_2_, ...), custom_call_target="tpu_custom_call" | custom-call | tf_op jit(solution)/shard_map/finish/pallas_call | solution.py:552
  (2 shorter events, 0.0 us)
Async XLA Ops:
  1.4 8.4 %collective-permute-start.1 = (bf16[32,4,128]{2,1,0:T(4,128)(2,1)S(1)}, bf16[32,4,128]{2,1,0:T(4,128)(2,1)S(1)}, u32[]{:S(2)}, u32[]{:S(2)}) collective-permute-start(bf16[32,4,128]{2,1,0:T(4,128)(2,1)S(1)} %bitcast.11), channel_id=1, source_target_pairs={{1,2},{3,4},{5,6},{7,8},{9,10},{11,12},{13,14},{15,16},{17,18},{19... | collective-permute-start | bytes 98312 | tf_op jit(solution)/shard_map/ppermute | solution.py:446
  2.1 7.7 %collective-permute-start = (bf16[32,4,128]{2,1,0:T(4,128)(2,1)S(1)}, bf16[32,4,128]{2,1,0:T(4,128)(2,1)S(1)}, u32[]{:S(2)}, u32[]{:S(2)}) collective-permute-start(bf16[32,4,128]{2,1,0:T(4,128)(2,1)S(1)} %bitcast.12), channel_id=1, source_target_pairs={{0,1},{2,3},{4,5},{6,7},{8,9},{10,11},{12,13},{14,15},{16,17},{18,... | collective-permute-start | bytes 98312 | tf_op jit(solution)/shard_map/ppermute | solution.py:447
  13.9 5.8 %collective-permute-start.3 = (bf16[32,4,128]{2,1,0:T(4,128)(2,1)S(1)}, bf16[32,4,128]{2,1,0:T(4,128)(2,1)S(1)}, u32[]{:S(2)}, u32[]{:S(2)}) collective-permute-start(bf16[32,4,128]{2,1,0:T(4,128)(2,1)S(1)} %get-tuple-element.38.mine), channel_id=1, source_target_pairs={{1,2},{3,4},{5,6},{7,8},{9,10},{11,12},{13,14},{15,16},{17,18},{19... | collective-permute-start | bytes 98312 | tf_op jit(solution)/shard_map/ppermute | solution.py:521
  14.6 5.1 %collective-permute-start.2 = (bf16[32,4,128]{2,1,0:T(4,128)(2,1)S(1)}, bf16[32,4,128]{2,1,0:T(4,128)(2,1)S(1)}, u32[]{:S(2)}, u32[]{:S(2)}) collective-permute-start(bf16[32,4,128]{2,1,0:T(4,128)(2,1)S(1)} %get-tuple-element.38.mine), channel_id=1, source_target_pairs={{0,1},{2,3},{4,5},{6,7},{8,9},{10,11},{12,13},{14,15},{16,17},{18,... | collective-permute-start | bytes 98312 | tf_op jit(solution)/shard_map/ppermute | solution.py:522
  22.0 1.3 %collective-permute-start.4 = (f32[72,128]{1,0:T(8,128)S(1)}, f32[72,128]{1,0:T(8,128)S(1)}, u32[]{:S(2)}, u32[]{:S(2)}) collective-permute-start(f32[72,128]{1,0:T(8,128)S(1)} %backward_outer.1), channel_id=1, source_target_pairs={{0,1},{1,0},{2,3},{3,2},{4,5},{5,4},{6,7},{7,6},{8,9},{9,8},{10,11... | collective-permute-start | bytes 110600 | tf_op jit(solution)/shard_map/ppermute | solution.py:546
  23.3 5.3 %collective-permute-start.7 = (f32[72,128]{1,0:T(8,128)S(1)}, f32[72,128]{1,0:T(8,128)S(1)}, u32[]{:S(2)}, u32[]{:S(2)}) collective-permute-start(f32[72,128]{1,0:T(8,128)S(1)} %add.12), channel_id=1, source_target_pairs={{0,6},{1,7},{2,4},{3,5},{4,2},{5,3},{6,0},{7,1},{8,14},{9,15},{10,... | collective-permute-start | bytes 110600 | tf_op jit(solution)/shard_map/ppermute | solution.py:546
  26.6 4.0 %collective-permute-start.6 = (f32[72,128]{1,0:T(8,128)S(1)}, f32[72,128]{1,0:T(8,128)S(1)}, u32[]{:S(2)}, u32[]{:S(2)}) collective-permute-start(f32[72,128]{1,0:T(8,128)S(1)} %add.12), channel_id=1, source_target_pairs={{0,4},{1,5},{2,6},{3,7},{4,0},{5,1},{6,2},{7,3},{8,12},{9,13},{10,... | collective-permute-start | bytes 110600 | tf_op jit(solution)/shard_map/ppermute | solution.py:546
  26.6 4.0 %collective-permute-start.5 = (f32[72,128]{1,0:T(8,128)S(1)}, f32[72,128]{1,0:T(8,128)S(1)}, u32[]{:S(2)}, u32[]{:S(2)}) collective-permute-start(f32[72,128]{1,0:T(8,128)S(1)} %add.12), channel_id=1, source_target_pairs={{0,2},{1,3},{2,0},{3,1},{4,6},{5,7},{6,4},{7,5},{8,10},{9,11},{10,... | collective-permute-start | bytes 110600 | tf_op jit(solution)/shard_map/ppermute | solution.py:546
  30.6 5.9 %collective-permute-start.10 = (f32[72,128]{1,0:T(8,128)S(1)}, f32[72,128]{1,0:T(8,128)S(1)}, u32[]{:S(2)}, u32[]{:S(2)}) collective-permute-start(f32[72,128]{1,0:T(8,128)S(1)} %add_add_fusion.refs_0_), channel_id=1, source_target_pairs={{0,24},{1,25},{2,26},{3,27},{4,28},{5,29},{6,30},{7,31},{8,16},{9,... | collective-permute-start | bytes 110600 | tf_op jit(solution)/shard_map/ppermute | solution.py:546
  33.9 4.9 %collective-permute-start.9 = (f32[72,128]{1,0:T(8,128)S(1)}, f32[72,128]{1,0:T(8,128)S(1)}, u32[]{:S(2)}, u32[]{:S(2)}) collective-permute-start(f32[72,128]{1,0:T(8,128)S(1)} %add_add_fusion.refs_0_), channel_id=1, source_target_pairs={{0,16},{1,17},{2,18},{3,19},{4,20},{5,21},{6,22},{7,23},{8,24},{9,... | collective-permute-start | bytes 110600 | tf_op jit(solution)/shard_map/ppermute | solution.py:546
  33.9 4.9 %collective-permute-start.8 = (f32[72,128]{1,0:T(8,128)S(1)}, f32[72,128]{1,0:T(8,128)S(1)}, u32[]{:S(2)}, u32[]{:S(2)}) collective-permute-start(f32[72,128]{1,0:T(8,128)S(1)} %add_add_fusion.refs_0_), channel_id=1, source_target_pairs={{0,8},{1,9},{2,10},{3,11},{4,12},{5,13},{6,14},{7,15},{8,0},{9,1},... | collective-permute-start | bytes 110600 | tf_op jit(solution)/shard_map/ppermute | solution.py:546
where the time goes:
time: 39.7 us; the launch traced here: 39.5 us
  starting transfers between devices  17.1 us (43%)
  Pallas kernels  12.6 us (32%)
  waiting for transfers between devices  8.25 us (21%)
  local copies, waits for them, and re-layouts  0.78 us (2%)
  between operations  0.73 us (2%)
    pallas_call x4, Pallas kernels, call(): pl.pallas_call(functools.partial(kernel, group, blocked), grid=grid, out_...  10.6 us
    ppermute x7, starting transfers between devices, local(): lax.ppermute(value, 'rec', [(s, s ^ k * at) for s in range(count)])  8.48 us
    ppermute x7, waiting for transfers between devices, local(): lax.ppermute(value, 'rec', [(s, s ^ k * at) for s in range(count)])  8.24 us
    ppermute x1, starting transfers between devices, local(): from_near = lax.ppermute(flat, 'rec', near)  4.36 us
    ppermute x1, starting transfers between devices, local(): g_near = lax.ppermute(g, 'rec', near)  2.9 us
    pallas_call x1, Pallas kernels, local(): pl.pallas_call(functools.partial(prep_kernel, blocks), out_shape=[jax.Sha...  1.29 us
  transfers between devices with their start and end apart: 11, of which 5 were waited for; matrix products, arithmetic and copies ran while one was open for 0% of the time, Pallas kernels for 14%

commit v1 on v0

--- a/solution.py
+++ b/solution.py
@@ -437,7 +437,7 @@
     group = group_of(count)
     steps = count // group
     width = group * 2 * samples
-    far = [(s, s + 1) for s in range(1, count - 1, 2)]
+    far = [(s, (s + 1) % count) for s in range(1, count, 2)]
     far += [(b, a) for a, b in far]
     near = [(s, s + 1) for s in range(0, count - 1, 2)]
     near += [(b, a) for a, b in near]

time: 39.7 us -> 39.9 us (level)
  starting transfers between devices: 17.1 us -> 18.1 us
  waiting for transfers between devices: 8.25 us -> 7.46 us
    ppermute x1, starting transfers between devices: 0.66 us -> 6.44 us  [local(): from_far = lax.ppermute(flat, 'rec', far)]
    ppermute x1, starting transfers between devices: 4.36 us -> 0.01 us  [local(): from_near = lax.ppermute(flat, 'rec', near)]
    ppermute x1, starting transfers between devices: 0.66 us -> 3.63 us  [local(): g_far = lax.ppermute(g, 'rec', far)]
    ppermute x1, starting transfers between devices: 2.9 us -> 0.01 us  [local(): g_near = lax.ppermute(g, 'rec', near)]
    ppermute x7, waiting for transfers between devices: 8.24 us -> 6.32 us  [local(): lax.ppermute(value, 'rec', [(s, s ^ k * at) for s in range(count)])]
    ppermute x1, waiting for transfers between devices: 0.01 us -> 1.13 us  [local(): g_far = lax.ppermute(g, 'rec', far)]
    ppermute x7, starting transfers between devices: 8.48 us -> 8 us  [local(): lax.ppermute(value, 'rec', [(s, s ^ k * at) for s in range(count)])]
  transfers between devices with their start and end apart: 11 -> 11, of which waited for: 5 -> 6; matrix products, arithmetic and copies ran while one was open for 0% -> 0% of each run, Pallas kernels for 14% -> 14%
where the time goes in v1:
time: 39.9 us; the launch traced here: 39.7 us
  starting transfers between devices  18.1 us (45%)
  Pallas kernels  12.6 us (32%)
  waiting for transfers between devices  7.46 us (19%)
  local copies, waits for them, and re-layouts  0.78 us (2%)
  between operations  0.72 us (2%)
    pallas_call x4, Pallas kernels, call(): pl.pallas_call(functools.partial(kernel, group, blocked), grid=grid, out_...  10.6 us
    ppermute x7, starting transfers between devices, local(): lax.ppermute(value, 'rec', [(s, s ^ k * at) for s in range(count)])  8 us
    ppermute x1, starting transfers between devices, local(): from_far = lax.ppermute(flat, 'rec', far)  6.44 us
    ppermute x7, waiting for transfers between devices, local(): lax.ppermute(value, 'rec', [(s, s ^ k * at) for s in range(count)])  6.32 us
    ppermute x1, starting transfers between devices, local(): g_far = lax.ppermute(g, 'rec', far)  3.63 us
    pallas_call x1, Pallas kernels, local(): pl.pallas_call(functools.partial(prep_kernel, blocks), out_shape=[jax.Sha...  1.29 us
    ppermute x1, waiting for transfers between devices, local(): g_far = lax.ppermute(g, 'rec', far)  1.13 us
  transfers between devices with their start and end apart: 11, of which 6 were waited for; matrix products, arithmetic and copies ran while one was open for 0% of the time, Pallas kernels for 14%

profile of v1, /device:TPU:0, one launch (start us, length us, event | category | flops | bytes accessed | tf_op | source)
XLA Modules:
  0.0 39.7 jit_solution(10064490701056532314)
XLA Ops:
  0.6 0.8 %copy.13 = bf16[16,2,4,128]{3,2,1,0:T(4,128)(2,1)S(1)} copy(bf16[16,2,4,128]{3,1,0,2:T(2,128)(2,1)} %bitcast.15) | data formatting | bytes 65536 | tf_op jit(solution)/shard_map/transpose | solution.py:445
  1.4 6.4 %collective-permute-start.1 = (bf16[32,4,128]{2,1,0:T(4,128)(2,1)S(1)}, bf16[32,4,128]{2,1,0:T(4,128)(2,1)S(1)}, u32[]{:S(2)}, u32[]{:S(2)}) collective-permute-start(bf16[32,4,128]{2,1,0:T(4,128)(2,1)S(1)} %bitcast.11), channel_id=1, source_target_pairs={{1,2},{3,4},{5,6},{7,8},{9,10},{11,12},{13,14},{15,16},{17,18},{19... | collective-permute-start | bytes 98312 | tf_op jit(solution)/shard_map/ppermute | solution.py:446
  7.8 0.0 collective-permute-start
  7.9 1.3 %prepare.1 = (s32[8,128]{1,0:T(8,128)S(1)}, bf16[64,48]{1,0:T(8,128)(2,1)S(1)}, bf16[64,80]{1,0:T(8,128)(2,1)S(1)}, bf16[24,192]{1,0:T(8,128)(2,1)S(1)}, bf16[64...) custom-call(s32[4,512]{1,0:T(4,128)} %bitcast.18, bf16[36,64]{1,0:T(8,128)(2,1)} %bitcast.16, f32[1,64]{1,0:T(1,128)} %bitcast.19, ...), custom_call_target="tpu_custom_call" | custom-call | tf_op jit(solution)/shard_map/prepare/pallas_call | solution.py:464
  9.1 2.0 %forward_inner.1 = (bf16[34,16,128]{2,1,0:T(8,128)(2,1)S(1)}, bf16[1,64,8192]{2,1,0:T(8,128)(2,1)S(1)}, bf16[1,64,8192]{2,1,0:T(8,128)(2,1)S(1)}, f32[1,64,8192]{2,1,0:T(8,128)S(1)}, f32[1,64,8192]{2,1,0:T(8,128)S(1)}) custom-call(s32[8,128]{1,0:T(8,128)S(1)} %get-tuple-element.31.slots, bf16[32,4,128]{2,1,0:T(4,128)(2,1)S(1)} %bitcast.13, ...), custom_call_target="tpu_custom_call" | custom-call | flops 201326592 | bytes 6291456 | tf_op jit(solution)/shard_map/forward_inner/pallas_call | solution.py:486
  11.2 0.0 collective-permute-done.1.far
  11.2 0.0 collective-permute-done.near
  11.2 4.1 %forward_outer.1 = (f32[4,16,2,128]{3,2,1,0:T(2,128)}, bf16[32,4,128]{2,1,0:T(4,128)(2,1)S(1)}, bf16[66,16,128]{2,1,0:T(8,128)(2,1)S(1)}, bf16[1,64,8192]{2,1,0:...) custom-call(s32[8,128]{1,0:T(8,128)S(1)} %get-tuple-element.31.slots, ...), custom_call_target="tpu_custom_call" | custom-call | flops 402653184 | bytes 12582912 | tf_op jit(solution)/shard_map/forward_outer/pallas_call | solution.py:486
  15.3 3.6 %collective-permute-start.3 = (bf16[32,4,128]{2,1,0:T(4,128)(2,1)S(1)}, bf16[32,4,128]{2,1,0:T(4,128)(2,1)S(1)}, u32[]{:S(2)}, u32[]{:S(2)}) collective-permute-start(bf16[32,4,128]{2,1,0:T(4,128)(2,1)S(1)} %get-tuple-element.38.mine), channel_id=1, source_target_pairs={{1,2},{3,4},{5,6},{7,8},{9,10},{11,12},{13,14},{15,16},{17,18},{19... | collective-permute-start | bytes 98312 | tf_op jit(solution)/shard_map/ppermute | solution.py:521
  18.9 0.0 collective-permute-start.2
  18.9 2.2 %backward_inner.1 = (bf16[34,16,128]{2,1,0:T(8,128)(2,1)S(1)}, f32[176,64]{1,0:T(8,128)S(1)}) custom-call(s32[8,128]{1,0:T(8,128)S(1)} %get-tuple-element.31.slots, bf16[32,4,128]{2,1,0:T(4,128)(2,1)S(1)} %get-tuple-element.38.mine, bf16[64,48]{1,0:T(8,128)(2,1)S(1)} %get-tuple-element.39.wo, bf16[64,64]{1,0:T(8,128)(2,1)S(1)} %get-tuple-element.40.wm, ...), custom_call_target="tpu_custom_call" | custom-call | flops 201326592 | bytes 6291456 | tf_op jit(solution)/shard_map/backward_inner/pallas_call | solution.py:486
  21.2 1.1 %collective-permute-done.3.far = bf16[32,4,128]{2,1,0:T(4,128)(2,1)S(1)} collective-permute-done((bf16[32,4,128]{2,1,0:T(4,128)(2,1)S(1)}, bf16[32,4,128]{2,1,0:T(4,128)(2,1)S(1)}, u32[]{:S(2)}, u32[]{:S(2)}) %collective-permute-start.3) | collective-permute-done | bytes 32800 | tf_op jit(solution)/shard_map/ppermute | solution.py:521
  22.3 0.0 collective-permute-done.2.near
  22.3 2.3 %backward_outer.1 = f32[72,128]{1,0:T(8,128)S(1)} custom-call(s32[8,128]{1,0:T(8,128)S(1)} %get-tuple-element.31.slots, bf16[32,4,128]{2,1,0:T(4,128)(2,1)S(1)} %collective-permute-done.2.near, bf16[32,4,128]{2,1,0:T(4,128)(2,1)S(1)} %collective-permute-done.3.far, bf16[64,48]{1,0:T(8,128)(2,1)S(1)} %get-tuple-element.39.wo, ...), custom_call_target="tpu_custom_call" | custom-call | flops 201326592 | bytes 6291456 | tf_op jit(solution)/shard_map/backward_outer/pallas_call | solution.py:486
  24.6 0.1 collective-permute-start.4
  24.7 1.2 %collective-permute-done.4 = f32[72,128]{1,0:T(8,128)S(1)} collective-permute-done((f32[72,128]{1,0:T(8,128)S(1)}, f32[72,128]{1,0:T(8,128)S(1)}, u32[]{:S(2)}, u32[]{:S(2)}) %collective-permute-start.4) | collective-permute-done | bytes 36896 | tf_op jit(solution)/shard_map/ppermute | solution.py:546
  25.9 0.0 collective-permute-start.7
  25.9 0.1 collective-permute-start.6
  26.0 3.4 %collective-permute-start.5 = (f32[72,128]{1,0:T(8,128)S(1)}, f32[72,128]{1,0:T(8,128)S(1)}, u32[]{:S(2)}, u32[]{:S(2)}) collective-permute-start(f32[72,128]{1,0:T(8,128)S(1)} %add.12), channel_id=1, source_target_pairs={{0,2},{1,3},{2,0},{3,1},{4,6},{5,7},{6,4},{7,5},{8,10},{9,11},{10,... | collective-permute-start | bytes 110600 | tf_op jit(solution)/shard_map/ppermute | solution.py:546
  29.4 1.4 %collective-permute-done.7 = f32[72,128]{1,0:T(8,128)S(1)} collective-permute-done((f32[72,128]{1,0:T(8,128)S(1)}, f32[72,128]{1,0:T(8,128)S(1)}, u32[]{:S(2)}, u32[]{:S(2)}) %collective-permute-start.7) | collective-permute-done | bytes 36896 | tf_op jit(solution)/shard_map/ppermute | solution.py:546
  30.7 0.0 collective-permute-done.6
  30.7 0.6 %collective-permute-done.5 = f32[72,128]{1,0:T(8,128)S(1)} collective-permute-done((f32[72,128]{1,0:T(8,128)S(1)}, f32[72,128]{1,0:T(8,128)S(1)}, u32[]{:S(2)}, u32[]{:S(2)}) %collective-permute-start.5) | collective-permute-done | bytes 36896 | tf_op jit(solution)/shard_map/ppermute | solution.py:546
  31.3 2.8 %collective-permute-start.10 = (f32[72,128]{1,0:T(8,128)S(1)}, f32[72,128]{1,0:T(8,128)S(1)}, u32[]{:S(2)}, u32[]{:S(2)}) collective-permute-start(f32[72,128]{1,0:T(8,128)S(1)} %add_add_fusion.refs_0_), channel_id=1, source_target_pairs={{0,24},{1,25},{2,26},{3,27},{4,28},{5,29},{6,30},{7,31},{8,16},{9,... | collective-permute-start | bytes 110600 | tf_op jit(solution)/shard_map/ppermute | solution.py:546
  34.1 0.0 collective-permute-start.9
  34.1 1.7 %collective-permute-start.8 = (f32[72,128]{1,0:T(8,128)S(1)}, f32[72,128]{1,0:T(8,128)S(1)}, u32[]{:S(2)}, u32[]{:S(2)}) collective-permute-start(f32[72,128]{1,0:T(8,128)S(1)} %add_add_fusion.refs_0_), channel_id=1, source_target_pairs={{0,8},{1,9},{2,10},{3,11},{4,12},{5,13},{6,14},{7,15},{8,0},{9,1},... | collective-permute-start | bytes 110600 | tf_op jit(solution)/shard_map/ppermute | solution.py:546
  35.8 1.4 %collective-permute-done.10.refs_3_ = f32[72,128]{1,0:T(8,128)S(1)} collective-permute-done((f32[72,128]{1,0:T(8,128)S(1)}, f32[72,128]{1,0:T(8,128)S(1)}, u32[]{:S(2)}, u32[]{:S(2)}) %collective-permute-start.10) | collective-permute-done | bytes 36896 | tf_op jit(solution)/shard_map/ppermute | solution.py:546
  37.1 1.8 %collective-permute-done.9.refs_2_ = f32[72,128]{1,0:T(8,128)S(1)} collective-permute-done((f32[72,128]{1,0:T(8,128)S(1)}, f32[72,128]{1,0:T(8,128)S(1)}, u32[]{:S(2)}, u32[]{:S(2)}) %collective-permute-start.9) | collective-permute-done | bytes 36896 | tf_op jit(solution)/shard_map/ppermute | solution.py:546
  39.0 0.0 collective-permute-done.8.refs_1_
  39.0 0.7 %finish.1 = (f32[36,64]{1,0:T(8,128)}, f32[1,64]{1,0:T(1,128)}, f32[64,64]{1,0:T(8,128)}, f32[1,64]{1,0:T(1,128)}, f32[36,64]{1,0:T(8,128)}) custom-call(f32[72,128]{1,0:T(8,128)S(1)} %add_add_fusion.refs_0_, f32[72,128]{1,0:T(8,128)S(1)} %collective-permute-done.8.refs_1_, f32[72,128]{1,0:T(8,128)S(1)} %collective-permute-done.9.refs_2_, ...), custom_call_target="tpu_custom_call" | custom-call | tf_op jit(solution)/shard_map/finish/pallas_call | solution.py:552
  (2 shorter events, 0.0 us)
Async XLA Ops:
  1.4 9.8 %collective-permute-start.1 = (bf16[32,4,128]{2,1,0:T(4,128)(2,1)S(1)}, bf16[32,4,128]{2,1,0:T(4,128)(2,1)S(1)}, u32[]{:S(2)}, u32[]{:S(2)}) collective-permute-start(bf16[32,4,128]{2,1,0:T(4,128)(2,1)S(1)} %bitcast.11), channel_id=1, source_target_pairs={{1,2},{3,4},{5,6},{7,8},{9,10},{11,12},{13,14},{15,16},{17,18},{19... | collective-permute-start | bytes 98312 | tf_op jit(solution)/shard_map/ppermute | solution.py:446
  7.8 3.4 %collective-permute-start = (bf16[32,4,128]{2,1,0:T(4,128)(2,1)S(1)}, bf16[32,4,128]{2,1,0:T(4,128)(2,1)S(1)}, u32[]{:S(2)}, u32[]{:S(2)}) collective-permute-start(bf16[32,4,128]{2,1,0:T(4,128)(2,1)S(1)} %bitcast.12), channel_id=1, source_target_pairs={{0,1},{2,3},{4,5},{6,7},{8,9},{10,11},{12,13},{14,15},{16,17},{18,... | collective-permute-start | bytes 98312 | tf_op jit(solution)/shard_map/ppermute | solution.py:447
  15.3 7.0 %collective-permute-start.3 = (bf16[32,4,128]{2,1,0:T(4,128)(2,1)S(1)}, bf16[32,4,128]{2,1,0:T(4,128)(2,1)S(1)}, u32[]{:S(2)}, u32[]{:S(2)}) collective-permute-start(bf16[32,4,128]{2,1,0:T(4,128)(2,1)S(1)} %get-tuple-element.38.mine), channel_id=1, source_target_pairs={{1,2},{3,4},{5,6},{7,8},{9,10},{11,12},{13,14},{15,16},{17,18},{19... | collective-permute-start | bytes 98312 | tf_op jit(solution)/shard_map/ppermute | solution.py:521
  18.9 3.4 %collective-permute-start.2 = (bf16[32,4,128]{2,1,0:T(4,128)(2,1)S(1)}, bf16[32,4,128]{2,1,0:T(4,128)(2,1)S(1)}, u32[]{:S(2)}, u32[]{:S(2)}) collective-permute-start(bf16[32,4,128]{2,1,0:T(4,128)(2,1)S(1)} %get-tuple-element.38.mine), channel_id=1, source_target_pairs={{0,1},{2,3},{4,5},{6,7},{8,9},{10,11},{12,13},{14,15},{16,17},{18,... | collective-permute-start | bytes 98312 | tf_op jit(solution)/shard_map/ppermute | solution.py:522
  24.6 1.3 %collective-permute-start.4 = (f32[72,128]{1,0:T(8,128)S(1)}, f32[72,128]{1,0:T(8,128)S(1)}, u32[]{:S(2)}, u32[]{:S(2)}) collective-permute-start(f32[72,128]{1,0:T(8,128)S(1)} %backward_outer.1), channel_id=1, source_target_pairs={{0,1},{1,0},{2,3},{3,2},{4,5},{5,4},{6,7},{7,6},{8,9},{9,8},{10,11... | collective-permute-start | bytes 110600 | tf_op jit(solution)/shard_map/ppermute | solution.py:546
  25.9 4.9 %collective-permute-start.7 = (f32[72,128]{1,0:T(8,128)S(1)}, f32[72,128]{1,0:T(8,128)S(1)}, u32[]{:S(2)}, u32[]{:S(2)}) collective-permute-start(f32[72,128]{1,0:T(8,128)S(1)} %add.12), channel_id=1, source_target_pairs={{0,6},{1,7},{2,4},{3,5},{4,2},{5,3},{6,0},{7,1},{8,14},{9,15},{10,... | collective-permute-start | bytes 110600 | tf_op jit(solution)/shard_map/ppermute | solution.py:546
  25.9 4.9 %collective-permute-start.6 = (f32[72,128]{1,0:T(8,128)S(1)}, f32[72,128]{1,0:T(8,128)S(1)}, u32[]{:S(2)}, u32[]{:S(2)}) collective-permute-start(f32[72,128]{1,0:T(8,128)S(1)} %add.12), channel_id=1, source_target_pairs={{0,4},{1,5},{2,6},{3,7},{4,0},{5,1},{6,2},{7,3},{8,12},{9,13},{10,... | collective-permute-start | bytes 110600 | tf_op jit(solution)/shard_map/ppermute | solution.py:546
  26.0 5.3 %collective-permute-start.5 = (f32[72,128]{1,0:T(8,128)S(1)}, f32[72,128]{1,0:T(8,128)S(1)}, u32[]{:S(2)}, u32[]{:S(2)}) collective-permute-start(f32[72,128]{1,0:T(8,128)S(1)} %add.12), channel_id=1, source_target_pairs={{0,2},{1,3},{2,0},{3,1},{4,6},{5,7},{6,4},{7,5},{8,10},{9,11},{10,... | collective-permute-start | bytes 110600 | tf_op jit(solution)/shard_map/ppermute | solution.py:546
  31.3 5.8 %collective-permute-start.10 = (f32[72,128]{1,0:T(8,128)S(1)}, f32[72,128]{1,0:T(8,128)S(1)}, u32[]{:S(2)}, u32[]{:S(2)}) collective-permute-start(f32[72,128]{1,0:T(8,128)S(1)} %add_add_fusion.refs_0_), channel_id=1, source_target_pairs={{0,24},{1,25},{2,26},{3,27},{4,28},{5,29},{6,30},{7,31},{8,16},{9,... | collective-permute-start | bytes 110600 | tf_op jit(solution)/shard_map/ppermute | solution.py:546
  34.1 4.9 %collective-permute-start.9 = (f32[72,128]{1,0:T(8,128)S(1)}, f32[72,128]{1,0:T(8,128)S(1)}, u32[]{:S(2)}, u32[]{:S(2)}) collective-permute-start(f32[72,128]{1,0:T(8,128)S(1)} %add_add_fusion.refs_0_), channel_id=1, source_target_pairs={{0,16},{1,17},{2,18},{3,19},{4,20},{5,21},{6,22},{7,23},{8,24},{9,... | collective-permute-start | bytes 110600 | tf_op jit(solution)/shard_map/ppermute | solution.py:546
  34.1 4.9 %collective-permute-start.8 = (f32[72,128]{1,0:T(8,128)S(1)}, f32[72,128]{1,0:T(8,128)S(1)}, u32[]{:S(2)}, u32[]{:S(2)}) collective-permute-start(f32[72,128]{1,0:T(8,128)S(1)} %add_add_fusion.refs_0_), channel_id=1, source_target_pairs={{0,8},{1,9},{2,10},{3,11},{4,12},{5,13},{6,14},{7,15},{8,0},{9,1},... | collective-permute-start | bytes 110600 | tf_op jit(solution)/shard_map/ppermute | solution.py:546

commit v2 on v1

--- a/solution.py
+++ b/solution.py
@@ -63,6 +63,14 @@
     return t, q, a
 
 
+def far_of(within, across):
+    size = math.gcd(lax.axis_size("rec"), 8)
+    at = lax.rem(lax.axis_index("rec"), size)
+    end = ((at == 0) | (at == size - 1)).astype(jnp.float32)
+    x, y = within[...].astype(jnp.float32), across[...].astype(jnp.float32)
+    return jnp.where(jnp.full(x.shape, end) > 0.0, y, x)
+
+
 def lines_of(idx, own, halo, owners):
     lines = []
     for e in owners:
@@ -136,7 +144,7 @@
 
 
 def forward_outer(
-    group, blocked, slots, near, mine, far, own, w1, w2, w3, inner,
+    group, blocked, slots, near, mine, far, across, own, w1, w2, w3, inner,
     res, g, halo, a1_ref, a2_ref, d1_ref, d2_ref, est, idx, sem,
 ):
     tiles, parts, samples = mine.shape
@@ -149,7 +157,7 @@
     high = (lane < samples - 1).astype(jnp.float32)
 
     def start():
-        fill_table(halo, (near, far), tiles, False, 1.0)
+        fill_table(halo, (near, far_of(far, across)), tiles, False, 1.0)
 
     def step(n, block):
         cut = lambda x, k: x[:, k * samples : (k + 1) * samples]
@@ -262,7 +270,7 @@
 
 
 def backward_outer(
-    group, blocked, slots, near, far, wo, wm, own, halo, gown, sums, a1_ref, a2_ref, d1_ref, d2_ref,
+    group, blocked, slots, near, far, across, wo, wm, own, halo, gown, sums, a1_ref, a2_ref, d1_ref, d2_ref,
     out, ghalo, acc, idx, sem,
 ):
     owners = lax.axis_size("rec")
@@ -270,7 +278,7 @@
     taps = 9 * near.shape[1]
 
     def start():
-        fill_table(ghalo, (near, far), near.shape[0], True, 0.0)
+        fill_table(ghalo, (near, far_of(far, across)), near.shape[0], True, 0.0)
         acc[...] = sums[...]
 
     def step(n, block):
@@ -437,13 +445,20 @@
     group = group_of(count)
     steps = count // group
     width = group * 2 * samples
-    far = [(s, (s + 1) % count) for s in range(1, count, 2)]
-    far += [(b, a) for a, b in far]
+    size = math.gcd(count, 8)
+    within = [(r + k, r + k + 1) for r in range(0, count, size) for k in range(1, size - 1, 2)]
+    within += [(r, r + size - 1) for r in range(0, count, size)]
+    within += [(b, a) for a, b in within]
+    across = [(r - 1 - k, r + k) for r in range(size, count, size) for k in range(2)]
+    taken = {s for pair in across for s in pair}
+    across += [(s, s + 1) for s in range(0, count, 2) if s not in taken]
+    across += [(b, a) for a, b in across]
     near = [(s, s + 1) for s in range(0, count - 1, 2)]
     near += [(b, a) for a, b in near]
 
     flat = records.transpose(1, 2, 0, 3).reshape(tiles, parts, samples)
-    from_far = lax.ppermute(flat, "rec", far)
+    from_across = lax.ppermute(flat, "rec", across)
+    from_within = lax.ppermute(flat, "rec", within)
     from_near = lax.ppermute(flat, "rec", near)
 
     f32, bf16 = jnp.float32, jnp.bfloat16
@@ -506,7 +521,7 @@
         (idx, flat, w1, w2), "forward_inner", 2,
     )
     res, g, halo, *outer = call(
-        forward_outer, (7, 1),
+        forward_outer, (8, 1),
         (
             [
                 jax.ShapeDtypeStruct(records.shape, f32),
@@ -516,18 +531,19 @@
             1,
         ),
         [pltpu.VMEM((count * 4, 8, samples), f32)],
-        (idx, from_near, flat, from_far, own, w1, w2, w3, inner[1]), "forward_outer", 4,
-    )
-    g_far = lax.ppermute(g, "rec", far)
+        (idx, from_near, flat, from_within, from_across, own, w1, w2, w3, inner[1]), "forward_outer", 4,
+    )
+    g_across = lax.ppermute(g, "rec", across)
+    g_within = lax.ppermute(g, "rec", within)
     g_near = lax.ppermute(g, "rec", near)
     gown, part = call(
         backward_inner, (4, 4), ([table(1, bf16), pltpu.VMEM(total, f32)], 0), [],
         (idx, g, wo, wm, own, *inner), "backward_inner", 2,
     )
     (sums,) = call(
-        backward_outer, (8, 4), ([jax.ShapeDtypeStruct((rows, 2 * channels), f32)], 0),
+        backward_outer, (9, 4), ([jax.ShapeDtypeStruct((rows, 2 * channels), f32)], 0),
         [table(2, bf16), pltpu.VMEM(total, f32)],
-        (idx, g_near, g_far, wo, wm, own, halo, gown, part, *outer), "backward_outer", 2,
+        (idx, g_near, g_within, g_across, wo, wm, own, halo, gown, part, *outer), "backward_outer", 2,
     )
 
     if count & (count - 1):

time: 39.9 us -> 38.1 us (0.955)
  waiting for transfers between devices: 7.46 us -> 6.21 us
  starting transfers between devices: 18.1 us -> 17.4 us
    ppermute x2 -> x4, starting transfers between devices: 10.1 us -> 8.91 us  [the longest x1 4.65 us: local(): from_within = lax.ppermute(flat, 'rec', within)]
    ppermute x2 -> x4, waiting for transfers between devices: 1.13 us -> 0.01 us  [the longest x1 0.01 us: local(): from_across = lax.ppermute(flat, 'rec', across)]
    ppermute x7, starting transfers between devices: 8 us -> 8.52 us  [local(): lax.ppermute(value, 'rec', [(s, s ^ k * at) for s in range(count)])]
  transfers between devices with their start and end apart: 11 -> 13, of which waited for: 6 -> 5; matrix products, arithmetic and copies ran while one was open for 0% -> 0% of each run, Pallas kernels for 14% -> 15%
where the time goes in v2:
time: 38.1 us; the launch traced here: 37.8 us
  starting transfers between devices  17.4 us (46%)
  Pallas kernels  12.7 us (33%)
  waiting for transfers between devices  6.21 us (16%)
  local copies, waits for them, and re-layouts  0.78 us (2%)
  between operations  0.74 us (2%)
    pallas_call x4, Pallas kernels, call(): pl.pallas_call(functools.partial(kernel, group, blocked), grid=grid, out_...  10.7 us
    ppermute x7, starting transfers between devices, local(): lax.ppermute(value, 'rec', [(s, s ^ k * at) for s in range(count)])  8.52 us
    ppermute x7, waiting for transfers between devices, local(): lax.ppermute(value, 'rec', [(s, s ^ k * at) for s in range(count)])  6.2 us
    ppermute x1, starting transfers between devices, local(): from_within = lax.ppermute(flat, 'rec', within)  4.65 us
    ppermute x1, starting transfers between devices, local(): g_within = lax.ppermute(g, 'rec', within)  3.14 us
    pallas_call x1, Pallas kernels, local(): pl.pallas_call(functools.partial(prep_kernel, blocks), out_shape=[jax.Sha...  1.29 us
    transpose x1, local copies, waits for them, and re-layouts, local(): flat = records.transpose(1, 2, 0, 3).reshape(tiles, parts, samples)  0.78 us
  transfers between devices with their start and end apart: 13, of which 5 were waited for; matrix products, arithmetic and copies ran while one was open for 0% of the time, Pallas kernels for 15%

profile of v2, /device:TPU:0, one launch (start us, length us, event | category | flops | bytes accessed | tf_op | source)
XLA Modules:
  0.0 37.8 jit_solution(3320677360655877282)
XLA Ops:
  0.6 0.8 %copy.13 = bf16[16,2,4,128]{3,2,1,0:T(4,128)(2,1)S(1)} copy(bf16[16,2,4,128]{3,1,0,2:T(2,128)(2,1)} %bitcast.16) | data formatting | bytes 65536 | tf_op jit(solution)/shard_map/transpose | solution.py:459
  1.4 0.5 %collective-permute-start.2 = (bf16[32,4,128]{2,1,0:T(4,128)(2,1)S(1)}, bf16[32,4,128]{2,1,0:T(4,128)(2,1)S(1)}, u32[]{:S(2)}, u32[]{:S(2)}) collective-permute-start(bf16[32,4,128]{2,1,0:T(4,128)(2,1)S(1)} %bitcast.11), channel_id=1, source_target_pairs={{7,8},{6,9},{15,16},{14,17},{23,24},{22,25},{0,1},{2,3},{4,5},{10,... | collective-permute-start | bytes 98312 | tf_op jit(solution)/shard_map/ppermute | solution.py:460
  1.9 4.7 %collective-permute-start.1 = (bf16[32,4,128]{2,1,0:T(4,128)(2,1)S(1)}, bf16[32,4,128]{2,1,0:T(4,128)(2,1)S(1)}, u32[]{:S(2)}, u32[]{:S(2)}) collective-permute-start(bf16[32,4,128]{2,1,0:T(4,128)(2,1)S(1)} %bitcast.12), channel_id=1, source_target_pairs={{1,2},{3,4},{5,6},{9,10},{11,12},{13,14},{17,18},{19,20},{21,22},{... | collective-permute-start | bytes 98312 | tf_op jit(solution)/shard_map/ppermute | solution.py:461
  6.6 0.0 collective-permute-start
  6.6 1.3 %prepare.1 = (s32[8,128]{1,0:T(8,128)S(1)}, bf16[64,48]{1,0:T(8,128)(2,1)S(1)}, bf16[64,80]{1,0:T(8,128)(2,1)S(1)}, bf16[24,192]{1,0:T(8,128)(2,1)S(1)}, bf16[64...) custom-call(s32[4,512]{1,0:T(4,128)} %bitcast.19, bf16[36,64]{1,0:T(8,128)(2,1)} %bitcast.17, f32[1,64]{1,0:T(1,128)} %bitcast.20, ...), custom_call_target="tpu_custom_call" | custom-call | tf_op jit(solution)/shard_map/prepare/pallas_call | solution.py:479
  7.9 2.0 %forward_inner.1 = (bf16[34,16,128]{2,1,0:T(8,128)(2,1)S(1)}, bf16[1,64,8192]{2,1,0:T(8,128)(2,1)S(1)}, bf16[1,64,8192]{2,1,0:T(8,128)(2,1)S(1)}, f32[1,64,8192]{2,1,0:T(8,128)S(1)}, f32[1,64,8192]{2,1,0:T(8,128)S(1)}) custom-call(s32[8,128]{1,0:T(8,128)S(1)} %get-tuple-element.31.slots, bf16[32,4,128]{2,1,0:T(4,128)(2,1)S(1)} %bitcast.14, ...), custom_call_target="tpu_custom_call" | custom-call | flops 201326592 | bytes 6291456 | tf_op jit(solution)/shard_map/forward_inner/pallas_call | solution.py:501
  9.9 0.0 collective-permute-done.2.across
  9.9 0.0 collective-permute-done.1.far
  10.0 0.0 collective-permute-done.near
  10.0 4.1 %forward_outer.1 = (f32[4,16,2,128]{3,2,1,0:T(2,128)}, bf16[32,4,128]{2,1,0:T(4,128)(2,1)S(1)}, bf16[66,16,128]{2,1,0:T(8,128)(2,1)S(1)}, bf16[1,64,8192]{2,1,0:...) custom-call(s32[8,128]{1,0:T(8,128)S(1)} %get-tuple-element.31.slots, ...), custom_call_target="tpu_custom_call" | custom-call | flops 402653184 | bytes 12582912 | tf_op jit(solution)/shard_map/forward_outer/pallas_call | solution.py:501
  14.1 0.6 %collective-permute-start.5 = (bf16[32,4,128]{2,1,0:T(4,128)(2,1)S(1)}, bf16[32,4,128]{2,1,0:T(4,128)(2,1)S(1)}, u32[]{:S(2)}, u32[]{:S(2)}) collective-permute-start(bf16[32,4,128]{2,1,0:T(4,128)(2,1)S(1)} %get-tuple-element.38.mine), channel_id=1, source_target_pairs={{7,8},{6,9},{15,16},{14,17},{23,24},{22,25},{0,1},{2,3},{4,5},{10,... | collective-permute-start | bytes 98312 | tf_op jit(solution)/shard_map/ppermute | solution.py:536
  14.7 3.1 %collective-permute-start.4 = (bf16[32,4,128]{2,1,0:T(4,128)(2,1)S(1)}, bf16[32,4,128]{2,1,0:T(4,128)(2,1)S(1)}, u32[]{:S(2)}, u32[]{:S(2)}) collective-permute-start(bf16[32,4,128]{2,1,0:T(4,128)(2,1)S(1)} %get-tuple-element.38.mine), channel_id=1, source_target_pairs={{1,2},{3,4},{5,6},{9,10},{11,12},{13,14},{17,18},{19,20},{21,22},{... | collective-permute-start | bytes 98312 | tf_op jit(solution)/shard_map/ppermute | solution.py:537
  17.8 0.0 collective-permute-start.3
  17.8 2.2 %backward_inner.1 = (bf16[34,16,128]{2,1,0:T(8,128)(2,1)S(1)}, f32[176,64]{1,0:T(8,128)S(1)}) custom-call(s32[8,128]{1,0:T(8,128)S(1)} %get-tuple-element.31.slots, bf16[32,4,128]{2,1,0:T(4,128)(2,1)S(1)} %get-tuple-element.38.mine, bf16[64,48]{1,0:T(8,128)(2,1)S(1)} %get-tuple-element.39.wo, bf16[64,64]{1,0:T(8,128)(2,1)S(1)} %get-tuple-element.40.wm, ...), custom_call_target="tpu_custom_call" | custom-call | flops 201326592 | bytes 6291456 | tf_op jit(solution)/shard_map/backward_inner/pallas_call | solution.py:501
  20.0 0.0 collective-permute-done.5.across
  20.0 0.0 collective-permute-done.4.far
  20.1 0.0 collective-permute-done.3.near
  20.1 2.3 %backward_outer.1 = f32[72,128]{1,0:T(8,128)S(1)} custom-call(s32[8,128]{1,0:T(8,128)S(1)} %get-tuple-element.31.slots, bf16[32,4,128]{2,1,0:T(4,128)(2,1)S(1)} %collective-permute-done.3.near, bf16[32,4,128]{2,1,0:T(4,128)(2,1)S(1)} %collective-permute-done.4.far, bf16[32,4,128]{2,1,0:T(4,128)(2,1)S(1)} %collective-permute-done.5.across, ...), custom_call_target="tpu_custom_call" | custom-call | flops 201326592 | bytes 6291456 | tf_op jit(solution)/shard_map/backward_outer/pallas_call | solution.py:501
  22.4 0.6 %collective-permute-start.6 = (f32[72,128]{1,0:T(8,128)S(1)}, f32[72,128]{1,0:T(8,128)S(1)}, u32[]{:S(2)}, u32[]{:S(2)}) collective-permute-start(f32[72,128]{1,0:T(8,128)S(1)} %backward_outer.1), channel_id=1, source_target_pairs={{0,1},{1,0},{2,3},{3,2},{4,5},{5,4},{6,7},{7,6},{8,9},{9,8},{10,11... | collective-permute-start | bytes 110600 | tf_op jit(solution)/shard_map/ppermute | solution.py:562
  23.0 0.9 %collective-permute-done.6 = f32[72,128]{1,0:T(8,128)S(1)} collective-permute-done((f32[72,128]{1,0:T(8,128)S(1)}, f32[72,128]{1,0:T(8,128)S(1)}, u32[]{:S(2)}, u32[]{:S(2)}) %collective-permute-start.6) | collective-permute-done | bytes 36896 | tf_op jit(solution)/shard_map/ppermute | solution.py:562
  23.8 1.9 %collective-permute-start.9 = (f32[72,128]{1,0:T(8,128)S(1)}, f32[72,128]{1,0:T(8,128)S(1)}, u32[]{:S(2)}, u32[]{:S(2)}) collective-permute-start(f32[72,128]{1,0:T(8,128)S(1)} %add.12), channel_id=1, source_target_pairs={{0,6},{1,7},{2,4},{3,5},{4,2},{5,3},{6,0},{7,1},{8,14},{9,15},{10,... | collective-permute-start | bytes 110600 | tf_op jit(solution)/shard_map/ppermute | solution.py:562
  25.7 0.0 collective-permute-start.8
  25.7 1.6 %collective-permute-start.7 = (f32[72,128]{1,0:T(8,128)S(1)}, f32[72,128]{1,0:T(8,128)S(1)}, u32[]{:S(2)}, u32[]{:S(2)}) collective-permute-start(f32[72,128]{1,0:T(8,128)S(1)} %add.12), channel_id=1, source_target_pairs={{0,2},{1,3},{2,0},{3,1},{4,6},{5,7},{6,4},{7,5},{8,10},{9,11},{10,... | collective-permute-start | bytes 110600 | tf_op jit(solution)/shard_map/ppermute | solution.py:562
  27.3 1.4 %collective-permute-done.9 = f32[72,128]{1,0:T(8,128)S(1)} collective-permute-done((f32[72,128]{1,0:T(8,128)S(1)}, f32[72,128]{1,0:T(8,128)S(1)}, u32[]{:S(2)}, u32[]{:S(2)}) %collective-permute-start.9) | collective-permute-done | bytes 36896 | tf_op jit(solution)/shard_map/ppermute | solution.py:562
  28.7 0.9 %collective-permute-done.8 = f32[72,128]{1,0:T(8,128)S(1)} collective-permute-done((f32[72,128]{1,0:T(8,128)S(1)}, f32[72,128]{1,0:T(8,128)S(1)}, u32[]{:S(2)}, u32[]{:S(2)}) %collective-permute-start.8) | collective-permute-done | bytes 36896 | tf_op jit(solution)/shard_map/ppermute | solution.py:562
  29.7 2.4 %collective-permute-start.12 = (f32[72,128]{1,0:T(8,128)S(1)}, f32[72,128]{1,0:T(8,128)S(1)}, u32[]{:S(2)}, u32[]{:S(2)}) collective-permute-start(f32[72,128]{1,0:T(8,128)S(1)} %add_add_fusion.refs_0_), channel_id=1, source_target_pairs={{0,24},{1,25},{2,26},{3,27},{4,28},{5,29},{6,30},{7,31},{8,16},{9,... | collective-permute-start | bytes 110600 | tf_op jit(solution)/shard_map/ppermute | solution.py:562
  32.1 0.7 %collective-permute-start.11 = (f32[72,128]{1,0:T(8,128)S(1)}, f32[72,128]{1,0:T(8,128)S(1)}, u32[]{:S(2)}, u32[]{:S(2)}) collective-permute-start(f32[72,128]{1,0:T(8,128)S(1)} %add_add_fusion.refs_0_), channel_id=1, source_target_pairs={{0,16},{1,17},{2,18},{3,19},{4,20},{5,21},{6,22},{7,23},{8,24},{9,... | collective-permute-start | bytes 110600 | tf_op jit(solution)/shard_map/ppermute | solution.py:562
  32.8 1.4 %collective-permute-start.10 = (f32[72,128]{1,0:T(8,128)S(1)}, f32[72,128]{1,0:T(8,128)S(1)}, u32[]{:S(2)}, u32[]{:S(2)}) collective-permute-start(f32[72,128]{1,0:T(8,128)S(1)} %add_add_fusion.refs_0_), channel_id=1, source_target_pairs={{0,8},{1,9},{2,10},{3,11},{4,12},{5,13},{6,14},{7,15},{8,0},{9,1},... | collective-permute-start | bytes 110600 | tf_op jit(solution)/shard_map/ppermute | solution.py:562
  34.1 1.8 %collective-permute-done.12.refs_3_ = f32[72,128]{1,0:T(8,128)S(1)} collective-permute-done((f32[72,128]{1,0:T(8,128)S(1)}, f32[72,128]{1,0:T(8,128)S(1)}, u32[]{:S(2)}, u32[]{:S(2)}) %collective-permute-start.12) | collective-permute-done | bytes 36896 | tf_op jit(solution)/shard_map/ppermute | solution.py:562
  35.9 1.2 %collective-permute-done.11.refs_2_ = f32[72,128]{1,0:T(8,128)S(1)} collective-permute-done((f32[72,128]{1,0:T(8,128)S(1)}, f32[72,128]{1,0:T(8,128)S(1)}, u32[]{:S(2)}, u32[]{:S(2)}) %collective-permute-start.11) | collective-permute-done | bytes 36896 | tf_op jit(solution)/shard_map/ppermute | solution.py:562
  37.1 0.0 collective-permute-done.10.refs_1_
  37.1 0.7 %finish.1 = (f32[36,64]{1,0:T(8,128)}, f32[1,64]{1,0:T(1,128)}, f32[64,64]{1,0:T(8,128)}, f32[1,64]{1,0:T(1,128)}, f32[36,64]{1,0:T(8,128)}) custom-call(f32[72,128]{1,0:T(8,128)S(1)} %add_add_fusion.refs_0_, f32[72,128]{1,0:T(8,128)S(1)} %collective-permute-done.10.refs_1_, f32[72,128]{1,0:T(8,128)S(1)} %collective-permute-done.11.refs_2_, ...), custom_call_target="tpu_custom_call" | custom-call | tf_op jit(solution)/shard_map/finish/pallas_call | solution.py:568
  (3 shorter events, 0.0 us)
Async XLA Ops:
  1.4 8.5 %collective-permute-start.2 = (bf16[32,4,128]{2,1,0:T(4,128)(2,1)S(1)}, bf16[32,4,128]{2,1,0:T(4,128)(2,1)S(1)}, u32[]{:S(2)}, u32[]{:S(2)}) collective-permute-start(bf16[32,4,128]{2,1,0:T(4,128)(2,1)S(1)} %bitcast.11), channel_id=1, source_target_pairs={{7,8},{6,9},{15,16},{14,17},{23,24},{22,25},{0,1},{2,3},{4,5},{10,... | collective-permute-start | bytes 98312 | tf_op jit(solution)/shard_map/ppermute | solution.py:460
  1.9 8.0 %collective-permute-start.1 = (bf16[32,4,128]{2,1,0:T(4,128)(2,1)S(1)}, bf16[32,4,128]{2,1,0:T(4,128)(2,1)S(1)}, u32[]{:S(2)}, u32[]{:S(2)}) collective-permute-start(bf16[32,4,128]{2,1,0:T(4,128)(2,1)S(1)} %bitcast.12), channel_id=1, source_target_pairs={{1,2},{3,4},{5,6},{9,10},{11,12},{13,14},{17,18},{19,20},{21,22},{... | collective-permute-start | bytes 98312 | tf_op jit(solution)/shard_map/ppermute | solution.py:461
  6.6 3.4 %collective-permute-start = (bf16[32,4,128]{2,1,0:T(4,128)(2,1)S(1)}, bf16[32,4,128]{2,1,0:T(4,128)(2,1)S(1)}, u32[]{:S(2)}, u32[]{:S(2)}) collective-permute-start(bf16[32,4,128]{2,1,0:T(4,128)(2,1)S(1)} %bitcast.13), channel_id=1, source_target_pairs={{0,1},{2,3},{4,5},{6,7},{8,9},{10,11},{12,13},{14,15},{16,17},{18,... | collective-permute-start | bytes 98312 | tf_op jit(solution)/shard_map/ppermute | solution.py:462
  14.1 6.0 %collective-permute-start.5 = (bf16[32,4,128]{2,1,0:T(4,128)(2,1)S(1)}, bf16[32,4,128]{2,1,0:T(4,128)(2,1)S(1)}, u32[]{:S(2)}, u32[]{:S(2)}) collective-permute-start(bf16[32,4,128]{2,1,0:T(4,128)(2,1)S(1)} %get-tuple-element.38.mine), channel_id=1, source_target_pairs={{7,8},{6,9},{15,16},{14,17},{23,24},{22,25},{0,1},{2,3},{4,5},{10,... | collective-permute-start | bytes 98312 | tf_op jit(solution)/shard_map/ppermute | solution.py:536
  14.7 5.4 %collective-permute-start.4 = (bf16[32,4,128]{2,1,0:T(4,128)(2,1)S(1)}, bf16[32,4,128]{2,1,0:T(4,128)(2,1)S(1)}, u32[]{:S(2)}, u32[]{:S(2)}) collective-permute-start(bf16[32,4,128]{2,1,0:T(4,128)(2,1)S(1)} %get-tuple-element.38.mine), channel_id=1, source_target_pairs={{1,2},{3,4},{5,6},{9,10},{11,12},{13,14},{17,18},{19,20},{21,22},{... | collective-permute-start | bytes 98312 | tf_op jit(solution)/shard_map/ppermute | solution.py:537
  17.8 2.2 %collective-permute-start.3 = (bf16[32,4,128]{2,1,0:T(4,128)(2,1)S(1)}, bf16[32,4,128]{2,1,0:T(4,128)(2,1)S(1)}, u32[]{:S(2)}, u32[]{:S(2)}) collective-permute-start(bf16[32,4,128]{2,1,0:T(4,128)(2,1)S(1)} %get-tuple-element.38.mine), channel_id=1, source_target_pairs={{0,1},{2,3},{4,5},{6,7},{8,9},{10,11},{12,13},{14,15},{16,17},{18,... | collective-permute-start | bytes 98312 | tf_op jit(solution)/shard_map/ppermute | solution.py:538
  22.4 1.4 %collective-permute-start.6 = (f32[72,128]{1,0:T(8,128)S(1)}, f32[72,128]{1,0:T(8,128)S(1)}, u32[]{:S(2)}, u32[]{:S(2)}) collective-permute-start(f32[72,128]{1,0:T(8,128)S(1)} %backward_outer.1), channel_id=1, source_target_pairs={{0,1},{1,0},{2,3},{3,2},{4,5},{5,4},{6,7},{7,6},{8,9},{9,8},{10,11... | collective-permute-start | bytes 110600 | tf_op jit(solution)/shard_map/ppermute | solution.py:562
  23.8 4.9 %collective-permute-start.9 = (f32[72,128]{1,0:T(8,128)S(1)}, f32[72,128]{1,0:T(8,128)S(1)}, u32[]{:S(2)}, u32[]{:S(2)}) collective-permute-start(f32[72,128]{1,0:T(8,128)S(1)} %add.12), channel_id=1, source_target_pairs={{0,6},{1,7},{2,4},{3,5},{4,2},{5,3},{6,0},{7,1},{8,14},{9,15},{10,... | collective-permute-start | bytes 110600 | tf_op jit(solution)/shard_map/ppermute | solution.py:562
  25.7 4.0 %collective-permute-start.8 = (f32[72,128]{1,0:T(8,128)S(1)}, f32[72,128]{1,0:T(8,128)S(1)}, u32[]{:S(2)}, u32[]{:S(2)}) collective-permute-start(f32[72,128]{1,0:T(8,128)S(1)} %add.12), channel_id=1, source_target_pairs={{0,4},{1,5},{2,6},{3,7},{4,0},{5,1},{6,2},{7,3},{8,12},{9,13},{10,... | collective-permute-start | bytes 110600 | tf_op jit(solution)/shard_map/ppermute | solution.py:562
  25.7 4.0 %collective-permute-start.7 = (f32[72,128]{1,0:T(8,128)S(1)}, f32[72,128]{1,0:T(8,128)S(1)}, u32[]{:S(2)}, u32[]{:S(2)}) collective-permute-start(f32[72,128]{1,0:T(8,128)S(1)} %add.12), channel_id=1, source_target_pairs={{0,2},{1,3},{2,0},{3,1},{4,6},{5,7},{6,4},{7,5},{8,10},{9,11},{10,... | collective-permute-start | bytes 110600 | tf_op jit(solution)/shard_map/ppermute | solution.py:562
  29.7 6.2 %collective-permute-start.12 = (f32[72,128]{1,0:T(8,128)S(1)}, f32[72,128]{1,0:T(8,128)S(1)}, u32[]{:S(2)}, u32[]{:S(2)}) collective-permute-start(f32[72,128]{1,0:T(8,128)S(1)} %add_add_fusion.refs_0_), channel_id=1, source_target_pairs={{0,24},{1,25},{2,26},{3,27},{4,28},{5,29},{6,30},{7,31},{8,16},{9,... | collective-permute-start | bytes 110600 | tf_op jit(solution)/shard_map/ppermute | solution.py:562
  32.1 5.0 %collective-permute-start.11 = (f32[72,128]{1,0:T(8,128)S(1)}, f32[72,128]{1,0:T(8,128)S(1)}, u32[]{:S(2)}, u32[]{:S(2)}) collective-permute-start(f32[72,128]{1,0:T(8,128)S(1)} %add_add_fusion.refs_0_), channel_id=1, source_target_pairs={{0,16},{1,17},{2,18},{3,19},{4,20},{5,21},{6,22},{7,23},{8,24},{9,... | collective-permute-start | bytes 110600 | tf_op jit(solution)/shard_map/ppermute | solution.py:562
  32.8 4.4 %collective-permute-start.10 = (f32[72,128]{1,0:T(8,128)S(1)}, f32[72,128]{1,0:T(8,128)S(1)}, u32[]{:S(2)}, u32[]{:S(2)}) collective-permute-start(f32[72,128]{1,0:T(8,128)S(1)} %add_add_fusion.refs_0_), channel_id=1, source_target_pairs={{0,8},{1,9},{2,10},{3,11},{4,12},{5,13},{6,14},{7,15},{8,0},{9,1},... | collective-permute-start | bytes 110600 | tf_op jit(solution)/shard_map/ppermute | solution.py:562

commit v3 on v2

--- a/solution.py
+++ b/solution.py
@@ -533,8 +533,8 @@
         [pltpu.VMEM((count * 4, 8, samples), f32)],
         (idx, from_near, flat, from_within, from_across, own, w1, w2, w3, inner[1]), "forward_outer", 4,
     )
+    g_within = lax.ppermute(g, "rec", within)
     g_across = lax.ppermute(g, "rec", across)
-    g_within = lax.ppermute(g, "rec", within)
     g_near = lax.ppermute(g, "rec", near)
     gown, part = call(
         backward_inner, (4, 4), ([table(1, bf16), pltpu.VMEM(total, f32)], 0), [],

time: 38.1 us -> 38.1 us (level)
  no operation moved by 1% of the time
where the time goes in v3:
time: 38.1 us; the launch traced here: 37.8 us
  starting transfers between devices  17.4 us (46%)
  Pallas kernels  12.7 us (33%)
  waiting for transfers between devices  6.2 us (16%)
  local copies, waits for them, and re-layouts  0.78 us (2%)
  between operations  0.74 us (2%)
    pallas_call x4, Pallas kernels, call(): pl.pallas_call(functools.partial(kernel, group, blocked), grid=grid, out_...  10.7 us
    ppermute x7, starting transfers between devices, local(): lax.ppermute(value, 'rec', [(s, s ^ k * at) for s in range(count)])  8.52 us
    ppermute x7, waiting for transfers between devices, local(): lax.ppermute(value, 'rec', [(s, s ^ k * at) for s in range(count)])  6.19 us
    ppermute x1, starting transfers between devices, local(): from_within = lax.ppermute(flat, 'rec', within)  4.65 us
    ppermute x1, starting transfers between devices, local(): g_within = lax.ppermute(g, 'rec', within)  3.16 us
    pallas_call x1, Pallas kernels, local(): pl.pallas_call(functools.partial(prep_kernel, blocks), out_shape=[jax.Sha...  1.29 us
    transpose x1, local copies, waits for them, and re-layouts, local(): flat = records.transpose(1, 2, 0, 3).reshape(tiles, parts, samples)  0.78 us
  transfers between devices with their start and end apart: 13, of which 5 were waited for; matrix products, arithmetic and copies ran while one was open for 0% of the time, Pallas kernels for 15%

profile of v3, /device:TPU:0, one launch (start us, length us, event | category | flops | bytes accessed | tf_op | source)
XLA Modules:
  0.0 37.8 jit_solution(3320677360655877282)
XLA Ops:
  0.6 0.8 %copy.13 = bf16[16,2,4,128]{3,2,1,0:T(4,128)(2,1)S(1)} copy(bf16[16,2,4,128]{3,1,0,2:T(2,128)(2,1)} %bitcast.16) | data formatting | bytes 65536 | tf_op jit(solution)/shard_map/transpose | solution.py:459
  1.4 0.5 %collective-permute-start.2 = (bf16[32,4,128]{2,1,0:T(4,128)(2,1)S(1)}, bf16[32,4,128]{2,1,0:T(4,128)(2,1)S(1)}, u32[]{:S(2)}, u32[]{:S(2)}) collective-permute-start(bf16[32,4,128]{2,1,0:T(4,128)(2,1)S(1)} %bitcast.11), channel_id=1, source_target_pairs={{7,8},{6,9},{15,16},{14,17},{23,24},{22,25},{0,1},{2,3},{4,5},{10,... | collective-permute-start | bytes 98312 | tf_op jit(solution)/shard_map/ppermute | solution.py:460
  1.9 4.7 %collective-permute-start.1 = (bf16[32,4,128]{2,1,0:T(4,128)(2,1)S(1)}, bf16[32,4,128]{2,1,0:T(4,128)(2,1)S(1)}, u32[]{:S(2)}, u32[]{:S(2)}) collective-permute-start(bf16[32,4,128]{2,1,0:T(4,128)(2,1)S(1)} %bitcast.12), channel_id=1, source_target_pairs={{1,2},{3,4},{5,6},{9,10},{11,12},{13,14},{17,18},{19,20},{21,22},{... | collective-permute-start | bytes 98312 | tf_op jit(solution)/shard_map/ppermute | solution.py:461
  6.6 0.0 collective-permute-start
  6.6 1.3 %prepare.1 = (s32[8,128]{1,0:T(8,128)S(1)}, bf16[64,48]{1,0:T(8,128)(2,1)S(1)}, bf16[64,80]{1,0:T(8,128)(2,1)S(1)}, bf16[24,192]{1,0:T(8,128)(2,1)S(1)}, bf16[64...) custom-call(s32[4,512]{1,0:T(4,128)} %bitcast.19, bf16[36,64]{1,0:T(8,128)(2,1)} %bitcast.17, f32[1,64]{1,0:T(1,128)} %bitcast.20, ...), custom_call_target="tpu_custom_call" | custom-call | tf_op jit(solution)/shard_map/prepare/pallas_call | solution.py:479
  7.9 2.1 %forward_inner.1 = (bf16[34,16,128]{2,1,0:T(8,128)(2,1)S(1)}, bf16[1,64,8192]{2,1,0:T(8,128)(2,1)S(1)}, bf16[1,64,8192]{2,1,0:T(8,128)(2,1)S(1)}, f32[1,64,8192]{2,1,0:T(8,128)S(1)}, f32[1,64,8192]{2,1,0:T(8,128)S(1)}) custom-call(s32[8,128]{1,0:T(8,128)S(1)} %get-tuple-element.31.slots, bf16[32,4,128]{2,1,0:T(4,128)(2,1)S(1)} %bitcast.14, ...), custom_call_target="tpu_custom_call" | custom-call | flops 201326592 | bytes 6291456 | tf_op jit(solution)/shard_map/forward_inner/pallas_call | solution.py:501
  9.9 0.0 collective-permute-done.2.across
  10.0 0.0 collective-permute-done.1.far
  10.0 0.0 collective-permute-done.near
  10.0 4.1 %forward_outer.1 = (f32[4,16,2,128]{3,2,1,0:T(2,128)}, bf16[32,4,128]{2,1,0:T(4,128)(2,1)S(1)}, bf16[66,16,128]{2,1,0:T(8,128)(2,1)S(1)}, bf16[1,64,8192]{2,1,0:...) custom-call(s32[8,128]{1,0:T(8,128)S(1)} %get-tuple-element.31.slots, ...), custom_call_target="tpu_custom_call" | custom-call | flops 402653184 | bytes 12582912 | tf_op jit(solution)/shard_map/forward_outer/pallas_call | solution.py:501
  14.1 0.6 %collective-permute-start.5 = (bf16[32,4,128]{2,1,0:T(4,128)(2,1)S(1)}, bf16[32,4,128]{2,1,0:T(4,128)(2,1)S(1)}, u32[]{:S(2)}, u32[]{:S(2)}) collective-permute-start(bf16[32,4,128]{2,1,0:T(4,128)(2,1)S(1)} %get-tuple-element.38.mine), channel_id=1, source_target_pairs={{7,8},{6,9},{15,16},{14,17},{23,24},{22,25},{0,1},{2,3},{4,5},{10,... | collective-permute-start | bytes 98312 | tf_op jit(solution)/shard_map/ppermute | solution.py:537
  14.7 3.2 %collective-permute-start.4 = (bf16[32,4,128]{2,1,0:T(4,128)(2,1)S(1)}, bf16[32,4,128]{2,1,0:T(4,128)(2,1)S(1)}, u32[]{:S(2)}, u32[]{:S(2)}) collective-permute-start(bf16[32,4,128]{2,1,0:T(4,128)(2,1)S(1)} %get-tuple-element.38.mine), channel_id=1, source_target_pairs={{1,2},{3,4},{5,6},{9,10},{11,12},{13,14},{17,18},{19,20},{21,22},{... | collective-permute-start | bytes 98312 | tf_op jit(solution)/shard_map/ppermute | solution.py:536
  17.8 0.0 collective-permute-start.3
  17.8 2.2 %backward_inner.1 = (bf16[34,16,128]{2,1,0:T(8,128)(2,1)S(1)}, f32[176,64]{1,0:T(8,128)S(1)}) custom-call(s32[8,128]{1,0:T(8,128)S(1)} %get-tuple-element.31.slots, bf16[32,4,128]{2,1,0:T(4,128)(2,1)S(1)} %get-tuple-element.38.mine, bf16[64,48]{1,0:T(8,128)(2,1)S(1)} %get-tuple-element.39.wo, bf16[64,64]{1,0:T(8,128)(2,1)S(1)} %get-tuple-element.40.wm, ...), custom_call_target="tpu_custom_call" | custom-call | flops 201326592 | bytes 6291456 | tf_op jit(solution)/shard_map/backward_inner/pallas_call | solution.py:501
  20.0 0.0 collective-permute-done.5.across
  20.0 0.0 collective-permute-done.4.far
  20.1 0.0 collective-permute-done.3.near
  20.1 2.3 %backward_outer.1 = f32[72,128]{1,0:T(8,128)S(1)} custom-call(s32[8,128]{1,0:T(8,128)S(1)} %get-tuple-element.31.slots, bf16[32,4,128]{2,1,0:T(4,128)(2,1)S(1)} %collective-permute-done.3.near, bf16[32,4,128]{2,1,0:T(4,128)(2,1)S(1)} %collective-permute-done.4.far, bf16[32,4,128]{2,1,0:T(4,128)(2,1)S(1)} %collective-permute-done.5.across, ...), custom_call_target="tpu_custom_call" | custom-call | flops 201326592 | bytes 6291456 | tf_op jit(solution)/shard_map/backward_outer/pallas_call | solution.py:501
  22.4 0.6 %collective-permute-start.6 = (f32[72,128]{1,0:T(8,128)S(1)}, f32[72,128]{1,0:T(8,128)S(1)}, u32[]{:S(2)}, u32[]{:S(2)}) collective-permute-start(f32[72,128]{1,0:T(8,128)S(1)} %backward_outer.1), channel_id=1, source_target_pairs={{0,1},{1,0},{2,3},{3,2},{4,5},{5,4},{6,7},{7,6},{8,9},{9,8},{10,11... | collective-permute-start | bytes 110600 | tf_op jit(solution)/shard_map/ppermute | solution.py:562
  23.0 0.9 %collective-permute-done.6 = f32[72,128]{1,0:T(8,128)S(1)} collective-permute-done((f32[72,128]{1,0:T(8,128)S(1)}, f32[72,128]{1,0:T(8,128)S(1)}, u32[]{:S(2)}, u32[]{:S(2)}) %collective-permute-start.6) | collective-permute-done | bytes 36896 | tf_op jit(solution)/shard_map/ppermute | solution.py:562
  23.8 1.9 %collective-permute-start.9 = (f32[72,128]{1,0:T(8,128)S(1)}, f32[72,128]{1,0:T(8,128)S(1)}, u32[]{:S(2)}, u32[]{:S(2)}) collective-permute-start(f32[72,128]{1,0:T(8,128)S(1)} %add.12), channel_id=1, source_target_pairs={{0,6},{1,7},{2,4},{3,5},{4,2},{5,3},{6,0},{7,1},{8,14},{9,15},{10,... | collective-permute-start | bytes 110600 | tf_op jit(solution)/shard_map/ppermute | solution.py:562
  25.7 1.6 %collective-permute-start.7 = (f32[72,128]{1,0:T(8,128)S(1)}, f32[72,128]{1,0:T(8,128)S(1)}, u32[]{:S(2)}, u32[]{:S(2)}) collective-permute-start(f32[72,128]{1,0:T(8,128)S(1)} %add.12), channel_id=1, source_target_pairs={{0,2},{1,3},{2,0},{3,1},{4,6},{5,7},{6,4},{7,5},{8,10},{9,11},{10,... | collective-permute-start | bytes 110600 | tf_op jit(solution)/shard_map/ppermute | solution.py:562
  27.3 1.4 %collective-permute-done.9 = f32[72,128]{1,0:T(8,128)S(1)} collective-permute-done((f32[72,128]{1,0:T(8,128)S(1)}, f32[72,128]{1,0:T(8,128)S(1)}, u32[]{:S(2)}, u32[]{:S(2)}) %collective-permute-start.9) | collective-permute-done | bytes 36896 | tf_op jit(solution)/shard_map/ppermute | solution.py:562
  28.7 0.9 %collective-permute-done.8 = f32[72,128]{1,0:T(8,128)S(1)} collective-permute-done((f32[72,128]{1,0:T(8,128)S(1)}, f32[72,128]{1,0:T(8,128)S(1)}, u32[]{:S(2)}, u32[]{:S(2)}) %collective-permute-start.8) | collective-permute-done | bytes 36896 | tf_op jit(solution)/shard_map/ppermute | solution.py:562
  29.7 0.0 collective-permute-done.7
  29.7 2.4 %collective-permute-start.12 = (f32[72,128]{1,0:T(8,128)S(1)}, f32[72,128]{1,0:T(8,128)S(1)}, u32[]{:S(2)}, u32[]{:S(2)}) collective-permute-start(f32[72,128]{1,0:T(8,128)S(1)} %add_add_fusion.refs_0_), channel_id=1, source_target_pairs={{0,24},{1,25},{2,26},{3,27},{4,28},{5,29},{6,30},{7,31},{8,16},{9,... | collective-permute-start | bytes 110600 | tf_op jit(solution)/shard_map/ppermute | solution.py:562
  32.1 0.7 %collective-permute-start.11 = (f32[72,128]{1,0:T(8,128)S(1)}, f32[72,128]{1,0:T(8,128)S(1)}, u32[]{:S(2)}, u32[]{:S(2)}) collective-permute-start(f32[72,128]{1,0:T(8,128)S(1)} %add_add_fusion.refs_0_), channel_id=1, source_target_pairs={{0,16},{1,17},{2,18},{3,19},{4,20},{5,21},{6,22},{7,23},{8,24},{9,... | collective-permute-start | bytes 110600 | tf_op jit(solution)/shard_map/ppermute | solution.py:562
  32.8 1.4 %collective-permute-start.10 = (f32[72,128]{1,0:T(8,128)S(1)}, f32[72,128]{1,0:T(8,128)S(1)}, u32[]{:S(2)}, u32[]{:S(2)}) collective-permute-start(f32[72,128]{1,0:T(8,128)S(1)} %add_add_fusion.refs_0_), channel_id=1, source_target_pairs={{0,8},{1,9},{2,10},{3,11},{4,12},{5,13},{6,14},{7,15},{8,0},{9,1},... | collective-permute-start | bytes 110600 | tf_op jit(solution)/shard_map/ppermute | solution.py:562
  34.2 1.7 %collective-permute-done.12.refs_3_ = f32[72,128]{1,0:T(8,128)S(1)} collective-permute-done((f32[72,128]{1,0:T(8,128)S(1)}, f32[72,128]{1,0:T(8,128)S(1)}, u32[]{:S(2)}, u32[]{:S(2)}) %collective-permute-start.12) | collective-permute-done | bytes 36896 | tf_op jit(solution)/shard_map/ppermute | solution.py:562
  35.9 1.2 %collective-permute-done.11.refs_2_ = f32[72,128]{1,0:T(8,128)S(1)} collective-permute-done((f32[72,128]{1,0:T(8,128)S(1)}, f32[72,128]{1,0:T(8,128)S(1)}, u32[]{:S(2)}, u32[]{:S(2)}) %collective-permute-start.11) | collective-permute-done | bytes 36896 | tf_op jit(solution)/shard_map/ppermute | solution.py:562
  37.1 0.0 collective-permute-done.10.refs_1_
  37.1 0.7 %finish.1 = (f32[36,64]{1,0:T(8,128)}, f32[1,64]{1,0:T(1,128)}, f32[64,64]{1,0:T(8,128)}, f32[1,64]{1,0:T(1,128)}, f32[36,64]{1,0:T(8,128)}) custom-call(f32[72,128]{1,0:T(8,128)S(1)} %add_add_fusion.refs_0_, f32[72,128]{1,0:T(8,128)S(1)} %collective-permute-done.10.refs_1_, f32[72,128]{1,0:T(8,128)S(1)} %collective-permute-done.11.refs_2_, ...), custom_call_target="tpu_custom_call" | custom-call | tf_op jit(solution)/shard_map/finish/pallas_call | solution.py:568
  (3 shorter events, 0.0 us)
Async XLA Ops:
  1.4 8.5 %collective-permute-start.2 = (bf16[32,4,128]{2,1,0:T(4,128)(2,1)S(1)}, bf16[32,4,128]{2,1,0:T(4,128)(2,1)S(1)}, u32[]{:S(2)}, u32[]{:S(2)}) collective-permute-start(bf16[32,4,128]{2,1,0:T(4,128)(2,1)S(1)} %bitcast.11), channel_id=1, source_target_pairs={{7,8},{6,9},{15,16},{14,17},{23,24},{22,25},{0,1},{2,3},{4,5},{10,... | collective-permute-start | bytes 98312 | tf_op jit(solution)/shard_map/ppermute | solution.py:460
  1.9 8.0 %collective-permute-start.1 = (bf16[32,4,128]{2,1,0:T(4,128)(2,1)S(1)}, bf16[32,4,128]{2,1,0:T(4,128)(2,1)S(1)}, u32[]{:S(2)}, u32[]{:S(2)}) collective-permute-start(bf16[32,4,128]{2,1,0:T(4,128)(2,1)S(1)} %bitcast.12), channel_id=1, source_target_pairs={{1,2},{3,4},{5,6},{9,10},{11,12},{13,14},{17,18},{19,20},{21,22},{... | collective-permute-start | bytes 98312 | tf_op jit(solution)/shard_map/ppermute | solution.py:461
  6.6 3.4 %collective-permute-start = (bf16[32,4,128]{2,1,0:T(4,128)(2,1)S(1)}, bf16[32,4,128]{2,1,0:T(4,128)(2,1)S(1)}, u32[]{:S(2)}, u32[]{:S(2)}) collective-permute-start(bf16[32,4,128]{2,1,0:T(4,128)(2,1)S(1)} %bitcast.13), channel_id=1, source_target_pairs={{0,1},{2,3},{4,5},{6,7},{8,9},{10,11},{12,13},{14,15},{16,17},{18,... | collective-permute-start | bytes 98312 | tf_op jit(solution)/shard_map/ppermute | solution.py:462
  14.1 6.0 %collective-permute-start.5 = (bf16[32,4,128]{2,1,0:T(4,128)(2,1)S(1)}, bf16[32,4,128]{2,1,0:T(4,128)(2,1)S(1)}, u32[]{:S(2)}, u32[]{:S(2)}) collective-permute-start(bf16[32,4,128]{2,1,0:T(4,128)(2,1)S(1)} %get-tuple-element.38.mine), channel_id=1, source_target_pairs={{7,8},{6,9},{15,16},{14,17},{23,24},{22,25},{0,1},{2,3},{4,5},{10,... | collective-permute-start | bytes 98312 | tf_op jit(solution)/shard_map/ppermute | solution.py:537
  14.7 5.4 %collective-permute-start.4 = (bf16[32,4,128]{2,1,0:T(4,128)(2,1)S(1)}, bf16[32,4,128]{2,1,0:T(4,128)(2,1)S(1)}, u32[]{:S(2)}, u32[]{:S(2)}) collective-permute-start(bf16[32,4,128]{2,1,0:T(4,128)(2,1)S(1)} %get-tuple-element.38.mine), channel_id=1, source_target_pairs={{1,2},{3,4},{5,6},{9,10},{11,12},{13,14},{17,18},{19,20},{21,22},{... | collective-permute-start | bytes 98312 | tf_op jit(solution)/shard_map/ppermute | solution.py:536
  17.8 2.2 %collective-permute-start.3 = (bf16[32,4,128]{2,1,0:T(4,128)(2,1)S(1)}, bf16[32,4,128]{2,1,0:T(4,128)(2,1)S(1)}, u32[]{:S(2)}, u32[]{:S(2)}) collective-permute-start(bf16[32,4,128]{2,1,0:T(4,128)(2,1)S(1)} %get-tuple-element.38.mine), channel_id=1, source_target_pairs={{0,1},{2,3},{4,5},{6,7},{8,9},{10,11},{12,13},{14,15},{16,17},{18,... | collective-permute-start | bytes 98312 | tf_op jit(solution)/shard_map/ppermute | solution.py:538
  22.4 1.4 %collective-permute-start.6 = (f32[72,128]{1,0:T(8,128)S(1)}, f32[72,128]{1,0:T(8,128)S(1)}, u32[]{:S(2)}, u32[]{:S(2)}) collective-permute-start(f32[72,128]{1,0:T(8,128)S(1)} %backward_outer.1), channel_id=1, source_target_pairs={{0,1},{1,0},{2,3},{3,2},{4,5},{5,4},{6,7},{7,6},{8,9},{9,8},{10,11... | collective-permute-start | bytes 110600 | tf_op jit(solution)/shard_map/ppermute | solution.py:562
  23.8 4.9 %collective-permute-start.9 = (f32[72,128]{1,0:T(8,128)S(1)}, f32[72,128]{1,0:T(8,128)S(1)}, u32[]{:S(2)}, u32[]{:S(2)}) collective-permute-start(f32[72,128]{1,0:T(8,128)S(1)} %add.12), channel_id=1, source_target_pairs={{0,6},{1,7},{2,4},{3,5},{4,2},{5,3},{6,0},{7,1},{8,14},{9,15},{10,... | collective-permute-start | bytes 110600 | tf_op jit(solution)/shard_map/ppermute | solution.py:562
  25.7 4.0 %collective-permute-start.8 = (f32[72,128]{1,0:T(8,128)S(1)}, f32[72,128]{1,0:T(8,128)S(1)}, u32[]{:S(2)}, u32[]{:S(2)}) collective-permute-start(f32[72,128]{1,0:T(8,128)S(1)} %add.12), channel_id=1, source_target_pairs={{0,4},{1,5},{2,6},{3,7},{4,0},{5,1},{6,2},{7,3},{8,12},{9,13},{10,... | collective-permute-start | bytes 110600 | tf_op jit(solution)/shard_map/ppermute | solution.py:562
  25.7 4.0 %collective-permute-start.7 = (f32[72,128]{1,0:T(8,128)S(1)}, f32[72,128]{1,0:T(8,128)S(1)}, u32[]{:S(2)}, u32[]{:S(2)}) collective-permute-start(f32[72,128]{1,0:T(8,128)S(1)} %add.12), channel_id=1, source_target_pairs={{0,2},{1,3},{2,0},{3,1},{4,6},{5,7},{6,4},{7,5},{8,10},{9,11},{10,... | collective-permute-start | bytes 110600 | tf_op jit(solution)/shard_map/ppermute | solution.py:562
  29.7 6.2 %collective-permute-start.12 = (f32[72,128]{1,0:T(8,128)S(1)}, f32[72,128]{1,0:T(8,128)S(1)}, u32[]{:S(2)}, u32[]{:S(2)}) collective-permute-start(f32[72,128]{1,0:T(8,128)S(1)} %add_add_fusion.refs_0_), channel_id=1, source_target_pairs={{0,24},{1,25},{2,26},{3,27},{4,28},{5,29},{6,30},{7,31},{8,16},{9,... | collective-permute-start | bytes 110600 | tf_op jit(solution)/shard_map/ppermute | solution.py:562
  32.1 5.1 %collective-permute-start.11 = (f32[72,128]{1,0:T(8,128)S(1)}, f32[72,128]{1,0:T(8,128)S(1)}, u32[]{:S(2)}, u32[]{:S(2)}) collective-permute-start(f32[72,128]{1,0:T(8,128)S(1)} %add_add_fusion.refs_0_), channel_id=1, source_target_pairs={{0,16},{1,17},{2,18},{3,19},{4,20},{5,21},{6,22},{7,23},{8,24},{9,... | collective-permute-start | bytes 110600 | tf_op jit(solution)/shard_map/ppermute | solution.py:562
  32.8 4.4 %collective-permute-start.10 = (f32[72,128]{1,0:T(8,128)S(1)}, f32[72,128]{1,0:T(8,128)S(1)}, u32[]{:S(2)}, u32[]{:S(2)}) collective-permute-start(f32[72,128]{1,0:T(8,128)S(1)} %add_add_fusion.refs_0_), channel_id=1, source_target_pairs={{0,8},{1,9},{2,10},{3,11},{4,12},{5,13},{6,14},{7,15},{8,0},{9,1},... | collective-permute-start | bytes 110600 | tf_op jit(solution)/shard_map/ppermute | solution.py:562
